TPU v7x, 128 devices: a whole 4x4x4 slice. The times are simulated.
128 devices in a mesh: dom: 32 (over y, x, core), band: 4 (over z).
Axes of the slice: x: 4, y: 4, z: 4, core: 2. Of those that a mesh axis runs over, the one named last changes fastest.
Arguments:
- block: float32 [64, 442368], P('band', 'dom')
- stiffness: float32 [343, 343], replicated
- cell_scale: float32 [2048], P('dom'), may hold values from 0.3 to 3
- potential: float32 [343, 2048], P(None, 'dom'), may hold values from 0.1 to 2
- cell_dofs: int32 [343, 2048], P(None, 'dom'), may hold values from 0 to 17919, as said below
- cell_count: int32 [32], P('dom'), may hold values from 32 to 64, as said below
- hang_rows: int32 [27648], P('dom'), may hold values from 0 to 13823, as said below
- hang_masters: int32 [4, 27648], P(None, 'dom'), may hold values from 0 to 13823, as said below
- hang_weights: float32 [4, 27648], P(None, 'dom'), may hold values from 0.1 to 0.6
Outputs:
- basis: float32 [64, 442368], P('band', 'dom')
Inputs may be any that keep to these rules, and one draw needn't show every extreme that they name: `cell_dofs`: each cell's 343 rows are distinct and lie within a window of 686 rows of the extended vector of 17920 rows. `cell_count`: every shard has at least 32 live cells; some shard has exactly 64. `hang_rows`: within a shard the hanging rows are distinct and none of them is a master. `hang_masters`: masters are owned rows of the same shard.
All inputs are finite; a program needn't handle non-finite values.
Results may differ from a plain program's by a relative error of at most 0.00026.
Values sent between devices are 32-bit elements; how exact they have to be, the bound alone decides.
No kernel may reach another device: no remote copies, remote signals or barrier semaphores. Data moves between devices by JAX's collectives and lax.ppermute only.
A program may use at most 192 MiB of HBM per device.

v0:
```python
import functools
import jax
import jax.numpy as jnp
from jax import lax
from jax.experimental import pallas as pl
from jax.experimental.pallas import tpu as pltpu
from jax.sharding import PartitionSpec as P

RIM = 2048
NODES = 343
HANG = 864
MASTERS = 4
LOC = 13824
CELLS = 64
S = 16
L = 128
EXT = LOC + 2 * RIM
NB = LOC // L
RB = RIM // L
NPAD = 384
NJ = NPAD // L
WIDE = 7
NARROW = 3
PACK = 72
PW = 2 * NPAD + L
GROUP = 16
RING = 4 * GROUP
SLOTS = 14 * GROUP
HPAD = 896
HB = HPAD // L
ME = MASTERS * HPAD
HE = 1024
E = ME + HE
QLO = 512
QB = QLO // L
QHI = 9
BIG = 1 << 20
CENTRE = 4.5
HALF = 3.5
F32 = jnp.float32
BF16 = jnp.bfloat16
I32 = jnp.int32
VLIM = 28 * 1024 * 1024
SMALL = 20 * 1024 * 1024
WHOLE = 64 * 1024 * 1024

VM = pl.BlockSpec(memory_space=pltpu.VMEM)
SM = pl.BlockSpec(memory_space=pltpu.SMEM)
HBM = pl.BlockSpec(memory_space=pltpu.HBM)
NT = (((1,), (1,)), ((), ()))


def inside(side):
    dom = lax.axis_index("dom")
    return dom > 0 if side == 0 else dom < lax.axis_size("dom") - 1


def iota(shape, dim):
    return lax.broadcasted_iota(I32, shape, dim)


def lanes(x, idx):
    return jnp.take_along_axis(x, idx, axis=1, mode="promise_in_bounds")


def nn(a, b):
    return jnp.dot(a, b, preferred_element_type=F32)


def nt(a, b):
    return lax.dot_general(a, b, NT, preferred_element_type=F32)


def split(x):
    hi = x.astype(BF16)
    return hi, (x - hi.astype(F32)).astype(BF16)


def at(b):
    return pl.ds(pl.multiple_of(b * L, L), L)


def one_hot(row, n):
    return (jnp.broadcast_to(row, (n, row.shape[1])) == iota((n, row.shape[1]), 0)).astype(F32)


def hang_tables(ent_ref, a_ref, b_ref, lhs_ref, oh_ref, pe_ref, src_ref, posr_ref, hq_ref, start_ref):
    for i in range(E // L):
        col = slice(i * L, (i + 1) * L)
        row = ent_ref[0:1, col]
        a_ref[:, col] = one_hot(row >> 7, L).astype(BF16)
        b_ref[:, col] = one_hot(row & 127, L).astype(BF16)
    flag = nt(a_ref[...], b_ref[...]) > 0.5
    flagb = flag.astype(F32).astype(BF16)
    tri = (iota((L, L), 0) < iota((L, L), 1)).astype(F32).astype(BF16)
    low = (iota((L, L), 1) < iota((L, L), 0)).astype(F32).astype(BF16)
    total = nn(flagb, jnp.ones((L, L), BF16))
    pos = (nn(flagb, tri) + nn(low, total.astype(BF16))).astype(I32)
    posr_ref[...] = jnp.where(flag, pos, -1)
    totrow = nt(jnp.ones((8, L), BF16), flagb)
    start_ref[...] = nn(totrow.astype(BF16), tri).astype(I32)
    ph = (pos >> 7).astype(F32).astype(BF16)
    plo = (pos & 127).astype(F32).astype(BF16)
    for i in range(E // L):
        col = slice(i * L, (i + 1) * L)
        ent = ent_ref[0:1, col]
        mask = a_ref[:, col].astype(F32)
        b = b_ref[:, col]
        hi = jnp.sum(nn(ph, b) * mask, axis=0, keepdims=True)
        lo = jnp.sum(nn(plo, b) * mask, axis=0, keepdims=True)
        pe = jnp.where(ent >= 0, hi.astype(I32) * L + lo.astype(I32), BIG)
        pe_ref[0:1, col] = pe
        oh_ref[:, col] = one_hot(pe & (QLO - 1), QLO).astype(BF16)
        qm = one_hot(pe // QLO, 16)
        lhs_ref[0:16, col] = qm.astype(BF16)
        lhs_ref[16:32, col] = (qm * (ent >> 7).astype(F32)).astype(BF16)
        lhs_ref[32:48, col] = (qm * (ent & 127).astype(F32)).astype(BF16)
        lhs_ref[48:64, col] = (qm if i >= ME // L else jnp.zeros_like(qm)).astype(BF16)
    res = nt(lhs_ref[...], oh_ref[...])
    cnt = res[0:16]
    den = jnp.maximum(cnt, 1.0)
    blk = (res[16:32] / den + 0.5).astype(I32)
    lo = (res[32:48] / den + 0.5).astype(I32)
    src = jnp.where(cnt > 0.5, blk * L + lo, -1)
    for q in range(QHI):
        for t in range(QB):
            src_ref[QB * q + t : QB * q + t + 1, :] = src[q : q + 1, t * L : (t + 1) * L]
    hq_ref[...] = res[48:64]


def zat(c):
    return pl.ds(pl.multiple_of((c // QB) * S, S), S), pl.ds(pl.multiple_of((c % QB) * L, L), L)


UNROLL = 12


def compress(read, z_ref, src_ref, start_ref):
    z_ref[...] = jnp.zeros_like(z_ref)

    def step(i, cur):
        for k in range(UNROLL):
            b = i * UNROLL + k
            y = read(b)
            c = start_ref[0, b] >> 7
            ahead = start_ref[0, b + 1] >> 7
            parts = []
            for t in range(2):
                row = jnp.broadcast_to(src_ref[pl.ds(c + t, 1), :], (S, L))
                parts.append(((row >> 7) == b, lanes(y, row & 127)))
            cur = jnp.where(parts[0][0], parts[0][1], cur)
            r, l = zat(c)
            z_ref[r, l] = cur
            after = jnp.where(parts[1][0], parts[1][1], 0.0)
            cur = jnp.where(ahead > c, after, cur)
        return cur

    cur = lax.fori_loop(0, NB // UNROLL, step, jnp.zeros((S, L), F32))
    r, l = zat(start_ref[0, NB] >> 7)
    z_ref[r, l] = cur


def expand(b, y, z_ref, posr_ref, start_ref):
    row = jnp.broadcast_to(posr_ref[pl.ds(b, 1), :], (S, L))
    c0 = start_ref[0, b] >> 7
    for t in range(2):
        c = c0 + t
        r, l = zat(c)
        y = jnp.where((row >> 7) == c, lanes(z_ref[r, l], row & 127), y)
    return y


def gather_entries(z_ref, oh_ref, pe_ref, g_ref, first, last):
    zz = jnp.concatenate(split(z_ref[...]), axis=0)
    n = QHI * S
    w = 256
    for i in range(first // w, last // w):
        col = slice(i * w, (i + 1) * w)
        g = nn(zz, oh_ref[:, col])
        q = jnp.broadcast_to(pe_ref[0:1, col] // QLO, (S, w))
        hi = g[0:S]
        lo = g[n : n + S]
        for h in range(1, QHI):
            m = q == h
            hi = jnp.where(m, g[h * S : (h + 1) * S], hi)
            lo = jnp.where(m, g[n + h * S : n + (h + 1) * S], lo)
        g_ref[:, col] = hi + lo


def scatter_entries(g_ref, oh_ref, pe_ref, lhs_ref, first, last):
    n = QHI * S
    for i in range(first // L, last // L):
        col = slice(i * L, (i + 1) * L)
        g = g_ref[:, col]
        hi = g.astype(BF16).astype(F32)
        lo = g - hi
        q = jnp.broadcast_to(pe_ref[0:1, col] // QLO, (S, L))
        for h in range(QHI):
            m = q == h
            lhs_ref[h * S : (h + 1) * S, col] = jnp.where(m, hi, 0.0).astype(BF16)
            lhs_ref[n + h * S : n + (h + 1) * S, col] = jnp.where(m, lo, 0.0).astype(BF16)
    res = nt(lhs_ref[:, first:last], oh_ref[:, first:last])
    return res[:n] + res[n:]


def hanging_values(z_ref, oh_ref, pe_ref, w_ref, g_ref, lhs_ref, hq_ref):
    gather_entries(z_ref, oh_ref, pe_ref, g_ref, 0, ME)
    g_ref[:, ME + HPAD :] = jnp.zeros((S, HE - HPAD), F32)
    for j in range(HB):
        acc = jnp.zeros((S, L), F32)
        for k in range(MASTERS):
            col = slice(k * HPAD + j * L, k * HPAD + (j + 1) * L)
            acc = acc + g_ref[:, col] * w_ref[0:1, col]
        g_ref[:, ME + j * L : ME + (j + 1) * L] = acc
    cz = scatter_entries(g_ref, oh_ref, pe_ref, lhs_ref, ME, E)
    for h in range(QHI):
        r = slice(h * S, (h + 1) * S)
        m = jnp.broadcast_to(hq_ref[h : h + 1, :], (S, QLO)) > 0.5
        z_ref[r, :] = jnp.where(m, cz[r], z_ref[r, :])


def add_to_masters(z_ref, oh_ref, pe_ref, w_ref, g_ref, lhs_ref):
    gather_entries(z_ref, oh_ref, pe_ref, g_ref, ME, E)
    for j in range(HB):
        y = g_ref[:, ME + j * L : ME + (j + 1) * L]
        for k in range(MASTERS):
            col = slice(k * HPAD + j * L, k * HPAD + (j + 1) * L)
            g_ref[:, col] = y * w_ref[0:1, col]
    z_ref[...] += scatter_entries(g_ref, oh_ref, pe_ref, lhs_ref, 0, ME)


def prepare_kernel(
    hang_ref, block_ref,
    pe_ref, w_ref, src_ref, posr_ref, hq_ref, start_ref, u_ref, left_ref, right_ref,
    ent_ref, oh_ref, a_ref, b_ref, tab_ref, z_ref, g_ref, lhs_ref, start_s, sem,
):
    for k in range(MASTERS):
        col = slice(k * HPAD, (k + 1) * HPAD)
        ent_ref[0:1, col] = hang_ref[k : k + 1, :].astype(I32)
        w_ref[0:1, col] = hang_ref[MASTERS + 1 + k : MASTERS + 2 + k, :]
    ent_ref[0:1, ME + HPAD :] = jnp.full((1, HE - HPAD), -1, I32)
    ent_ref[0:1, ME : ME + HPAD] = hang_ref[MASTERS : MASTERS + 1, :].astype(I32)
    hang_tables(ent_ref, a_ref, b_ref, tab_ref, oh_ref, pe_ref, src_ref, posr_ref, hq_ref, start_ref)
    copy = pltpu.make_async_copy(start_ref, start_s, sem)
    copy.start()
    copy.wait()
    compress(lambda b: block_ref[:, at(b)], z_ref, src_ref, start_s)
    hanging_values(z_ref, oh_ref, pe_ref, w_ref, g_ref, lhs_ref, hq_ref)

    def step(i, _):
        for k in range(UNROLL):
            b = i * UNROLL + k
            u_ref[:, at(b)] = expand(b, block_ref[:, at(b)], z_ref, posr_ref, start_s)
        return 0

    lax.fori_loop(0, NB // UNROLL, step, 0)
    left_ref[...] = u_ref[:, 0:RIM]
    right_ref[...] = u_ref[:, LOC - RIM :]


def sds(shape, dtype=F32):
    return jax.ShapeDtypeStruct(shape, dtype)


HANG_SCRATCH = [
    pltpu.VMEM((QHI * S, QLO), F32),
    pltpu.VMEM((S, E), F32),
    pltpu.VMEM((2 * QHI * S, E), BF16),
]


def prepare(hang, block):
    return pl.pallas_call(
        prepare_kernel,
        out_shape=(
            sds((1, E), I32),
            sds((1, ME)),
            sds((QB * QHI + 4, L), I32),
            sds((L, L), I32),
            sds((16, QLO)),
            sds((8, L), I32),
            sds((S, LOC)),
            sds((S, RIM)),
            sds((S, RIM)),
        ),
        in_specs=[VM] * 2,
        out_specs=(VM,) * 9,
        scratch_shapes=[
            pltpu.VMEM((1, E), I32),
            pltpu.VMEM((QLO, E), BF16),
            pltpu.VMEM((L, E), BF16),
            pltpu.VMEM((L, E), BF16),
            pltpu.VMEM((64, E), BF16),
            *HANG_SCRATCH,
            pltpu.SMEM((8, L), I32),
            pltpu.SemaphoreType.DMA,
        ],
        compiler_params=pltpu.CompilerParams(vmem_limit_bytes=VLIM),
        name="prepare",
    )(hang, block)


def pack_kernel(
    dofs_hbm, pot_hbm, scale_hbm, rows_hbm, masters_hbm, weights_hbm, count_ref,
    own_ref, hang_ref,
    dofs_ref, pot_ref, scale_ref, rows_ref, masters_ref, weights_ref, sems,
):
    moves = (
        (dofs_hbm, dofs_ref),
        (pot_hbm, pot_ref),
        (scale_hbm, scale_ref),
        (rows_hbm, rows_ref),
        (masters_hbm, masters_ref),
        (weights_hbm, weights_ref),
    )
    loads = [pltpu.make_async_copy(src, dst, sems.at[i]) for i, (src, dst) in enumerate(moves)]
    for load in loads:
        load.start()
    for load in loads:
        load.wait()
    own_ref[0:CELLS, 0:NODES] = dofs_ref[...].astype(F32)
    own_ref[0:CELLS, NPAD : NPAD + NODES] = pot_ref[...]
    scale = jnp.broadcast_to(scale_ref[...].reshape(1, CELLS), (PACK - CELLS, CELLS))
    own_ref[CELLS:PACK, 0:CELLS] = scale
    own_ref[CELLS:PACK, L : 2 * L] = jnp.full((PACK - CELLS, L), count_ref[0]).astype(F32)
    hang_ref[...] = jnp.where(iota((2 * MASTERS + 1, HPAD), 0) < MASTERS + 1, -1.0, 0.0)
    hang_ref[0:MASTERS, 0:HANG] = masters_ref[...].astype(F32)
    hang_ref[MASTERS : MASTERS + 1, 0:HANG] = rows_ref[...].reshape(1, HANG).astype(F32)
    hang_ref[MASTERS + 1 :, 0:HANG] = weights_ref[...]


def pack(dofs, pot, scale, rows, masters, weights, count):
    return pl.pallas_call(
        pack_kernel,
        out_shape=(sds((PACK, PW)), sds((2 * MASTERS + 1, HPAD))),
        in_specs=[HBM] * 6 + [SM],
        out_specs=(VM, VM),
        scratch_shapes=[
            pltpu.VMEM((CELLS, NODES), I32),
            pltpu.VMEM((CELLS, NODES), F32),
            pltpu.VMEM((CELLS,), F32),
            pltpu.VMEM((HANG,), I32),
            pltpu.VMEM((MASTERS, HANG), I32),
            pltpu.VMEM((MASTERS, HANG), F32),
            pltpu.SemaphoreType.DMA((6,)),
        ],
        compiler_params=pltpu.CompilerParams(vmem_limit_bytes=WHOLE),
        name="pack",
    )(dofs, pot, scale, rows, masters, weights, count)


def inverse(rels):
    oh = jnp.concatenate([one_hot(rel & 127, L) for rel in rels], axis=1).astype(BF16)
    rows = []
    for j, rel in enumerate(rels):
        m = jnp.broadcast_to(rel >> 7, (8, L)) == iota((8, L), 0)
        node = jnp.where(m, iota((8, L), 1) + 1, 0).astype(F32)
        zero = jnp.zeros((8, L), F32)
        rows.append(jnp.concatenate([node if i == j else zero for i in range(len(rels))], axis=1))
    return nt(jnp.concatenate(rows, axis=0).astype(BF16), oh).astype(I32) - 1


def cells_kernel(
    own_ref, left_ref, right_ref, pe_ref, k_hbm,
    tab_ref, pot_ref, kh_ref, kl_ref, oh_ref, base_ref,
    all_ref, meta_ref, k_ref, pad_ref, meta_s, list_s, wide_s, sem, sem_k,
):
    load = pltpu.make_async_copy(k_hbm, k_ref, sem_k)
    load.start()
    lane = iota((CELLS, L), 1)
    cell = iota((CELLS, L), 0)
    tail = NODES - 2 * L
    sources = ((own_ref, 0, None), (left_ref, -LOC, 0), (right_ref, LOC, 1))
    for i, (ref, shift, side) in enumerate(sources):
        r = slice(i * CELLS, (i + 1) * CELLS)
        lows, tops = [], []
        for j in range(NJ):
            dofs = ref[0:CELLS, j * L : (j + 1) * L] + float(shift)
            real = lane < (L if j < 2 else tail)
            low = jnp.where(real, dofs, float(BIG))
            all_ref[r, j * L : (j + 1) * L] = low
            pot = ref[0:CELLS, NPAD + j * L : NPAD + (j + 1) * L]
            all_ref[r, NPAD + j * L : NPAD + (j + 1) * L] = jnp.where(real, pot, 0.0)
            lows.append(jnp.min(low, axis=1, keepdims=True).astype(I32))
            tops.append(jnp.max(jnp.where(real, dofs, -float(BIG)), axis=1, keepdims=True).astype(I32))
        scales = jnp.broadcast_to(ref[CELLS : CELLS + 1, 0:L], (CELLS, L))
        scale = jnp.sum(jnp.where(lane == cell, scales, 0.0), axis=1, keepdims=True)
        all_ref[r, 2 * NPAD :] = jnp.broadcast_to(scale, (CELLS, L))
        count = jnp.broadcast_to(ref[CELLS : CELLS + 1, L : 2 * L], (CELLS, L))
        live = cell.astype(F32) < count
        if side is not None:
            live = live & jnp.full((CELLS, L), inside(side))
        low = jnp.minimum(jnp.minimum(lows[0], lows[1]), lows[2])
        top = jnp.maximum(jnp.maximum(tops[0], tops[1]), tops[2])
        used = live & (top >= RIM) & (low < RIM + LOC)
        starts = [jnp.minimum(x >> 7, EXT // L - NARROW) for x in lows]
        narrow = ((tops[0] >> 7) - starts[0] < NARROW) & ((tops[1] >> 7) - starts[1] < NARROW)
        narrow = narrow & ((tops[2] >> 7) - starts[2] < NARROW)
        base = jnp.minimum(low >> 7, EXT // L - WIDE)
        meta = jnp.where(used, jnp.where(narrow, 0, 1), -1)
        for j in range(NJ):
            meta = jnp.where(lane == 1 + j, jnp.where(narrow, starts[j], base), meta)
        meta_ref[r, :] = meta
    copy = pltpu.make_async_copy(meta_ref, meta_s, sem)
    copy.start()
    pad_ref[...] = jnp.zeros_like(pad_ref)
    load.wait()
    pad_ref[0:NODES, 0:NODES] = k_ref[...]
    kh_ref[...], kl_ref[...] = split(pad_ref[...])
    for i in range(E // L):
        col = slice(i * L, (i + 1) * L)
        oh_ref[:, col] = one_hot(pe_ref[0:1, col] & (QLO - 1), QLO).astype(BF16)
    copy.wait()

    def scan(c, counts):
        kind = meta_s[c, 0]
        n, m = counts
        list_s[n] = c
        wide_s[m] = c
        return n + jnp.where(kind == 0, 1, 0), m + jnp.where(kind == 1, 1, 0)

    n, m = lax.fori_loop(0, 3 * CELLS, scan, (0, 0), unroll=4)
    gn = (n + GROUP - 1) // GROUP
    gw = (m + GROUP - 1) // GROUP
    first = (gn + 1) * GROUP
    last = first + gw * GROUP

    def blank(i, _):
        list_s[i] = -1
        return 0

    def move(i, _):
        list_s[first + i] = wide_s[i]
        return 0

    lax.fori_loop(n, first, blank, 0)
    lax.fori_loop(0, m, move, 0)
    lax.fori_loop(first + m, last, blank, 0)
    base_ref[4 * SLOTS] = gn
    base_ref[4 * SLOTS + 1] = gw

    def one(slot):
        c = list_s[slot]
        valid = c >= 0
        c = jnp.maximum(c, 0)
        vals = all_ref[pl.ds(c, 1), :]
        rels = []
        for j in range(NJ):
            b = jnp.where(valid, meta_s[c, 1 + j], 0)
            base_ref[4 * slot + j] = b
            rel = vals[:, j * L : (j + 1) * L].astype(I32) - b * L
            rel = jnp.where(valid & (rel < WIDE * L), rel, BIG)
            rels.append(rel)
            tab_ref[slot, j : j + 1, :] = rel
            pot_ref[slot, j : j + 1, :] = vals[:, NPAD + j * L : NPAD + (j + 1) * L]
        pot_ref[slot, 3:4, :] = vals[:, 2 * NPAD :]
        inv = inverse(rels)
        for j in range(NJ):
            tab_ref[slot, 3 + 3 * j : 6 + 3 * j, :] = inv[8 * j : 8 * j + NARROW]

    def some(i, _):
        for k in range(8):
            one(i * 8 + k)
        return 0

    lax.fori_loop(0, last // 8, some, 0)


def cell_tables(own, left, right, pe, stiffness):
    return pl.pallas_call(
        cells_kernel,
        out_shape=(
            sds((SLOTS, 16, L), I32),
            sds((SLOTS, 8, L)),
            sds((NPAD, NPAD), BF16),
            sds((NPAD, NPAD), BF16),
            sds((QLO, E), BF16),
            sds((4 * SLOTS + L,), I32),
        ),
        in_specs=[VM] * 4 + [HBM],
        out_specs=(VM, VM, VM, VM, VM, SM),
        scratch_shapes=[
            pltpu.VMEM((3 * CELLS, PW), F32),
            pltpu.VMEM((3 * CELLS, L), I32),
            pltpu.VMEM((NODES, NODES), F32),
            pltpu.VMEM((NPAD, NPAD), F32),
            pltpu.SMEM((3 * CELLS, L), I32),
            pltpu.SMEM((SLOTS + GROUP,), I32),
            pltpu.SMEM((3 * CELLS + GROUP,), I32),
            pltpu.SemaphoreType.DMA,
            pltpu.SemaphoreType.DMA,
        ],
        compiler_params=pltpu.CompilerParams(vmem_limit_bytes=SMALL),
        name="cell_tables",
    )(own, left, right, pe, stiffness)


def step_kernel(number, *refs):
    (u_ref, gl_ref, gr_ref, prev_ref, tab_ref, pot_ref, kh_ref, kl_ref,
     oh_ref, pe_ref, w_ref, src_ref, posr_ref, hq_ref, base_ref, start_ref) = refs[:16]
    outs = refs[16 : 16 + (4 if number == 3 else 3)]
    ext_ref, acc0_ref, acc1_ref, x_ref, p_ref, z_ref, g_ref, lhs_ref = refs[16 + len(outs) :]
    accs = (acc0_ref, acc1_ref)
    ext_ref[:, 0:RIM] = jnp.where(inside(0), gl_ref[...], 0.0)
    ext_ref[:, RIM : RIM + LOC] = u_ref[...]
    ext_ref[:, RIM + LOC :] = jnp.where(inside(1), gr_ref[...], 0.0)
    for ref in accs:
        ref[...] = jnp.zeros_like(ref)
    gn = base_ref[4 * SLOTS]
    gw = base_ref[4 * SLOTS + 1]

    def load(slot, width):
        for j in range(NJ):
            b = base_ref[4 * slot + j]
            row = jnp.broadcast_to(tab_ref[slot, j : j + 1, :], (8, L))
            lo, hi = row & 127, row >> 7
            for s in range(2):
                r = slice(8 * s, 8 * s + 8)
                acc = lanes(ext_ref[r, at(b)], lo)
                for t in range(1, width):
                    acc = jnp.where(hi == t, lanes(ext_ref[r, at(b + t)], lo), acc)
                x_ref[pl.ds(pl.multiple_of((slot & (RING - 1)) * S + 8 * s, 8), 8), j * L : (j + 1) * L] = acc

    def store(slot, parity, width):
        acc_ref = accs[parity]
        scale = jnp.broadcast_to(pot_ref[slot, 3:4, :], (8, L))
        if width == NARROW:
            inv = [[tab_ref[slot, 3 + 3 * j + t : 4 + 3 * j + t, :] for t in range(width)] for j in range(NJ)]
        else:
            full = inverse([tab_ref[slot, j : j + 1, :] for j in range(NJ)])
            inv = [[full[8 * j + t : 8 * j + t + 1] for t in range(width)] for j in range(NJ)]
        for j in range(NJ):
            b = base_ref[4 * slot + j]
            col = slice(j * L, (j + 1) * L)
            pot = jnp.broadcast_to(pot_ref[slot, j : j + 1, :], (8, L))
            vals = []
            for s in range(2):
                r = pl.ds(pl.multiple_of((slot & (RING - 1)) * S + 8 * s, 8), 8)
                vals.append(scale * p_ref[r, col] + pot * x_ref[r, col])
            adds = []
            for t in range(width):
                row = jnp.broadcast_to(inv[j][t], (8, L))
                m, lo = row >= 0, row & 127
                adds.append([jnp.where(m, lanes(vals[s], lo), 0.0) for s in range(2)])
            olds = [[acc_ref[8 * s : 8 * s + 8, at(b + t)] for s in range(2)] for t in range(width)]
            for t in range(width):
                for s in range(2):
                    acc_ref[8 * s : 8 * s + 8, at(b + t)] = olds[t][s] + adds[t][s]

    def rows_of(i):
        return pl.ds(pl.multiple_of((i & 3) * (GROUP * S), GROUP * S), GROUP * S)

    def product(i):
        xh, xl = split(x_ref[rows_of(i), :])
        kh, kl = kh_ref[...], kl_ref[...]
        return nt(xh, kh) + (nt(xl, kh) + nt(xh, kl))

    def load_group(i, width, n):
        def some(q, _):
            for k in range(n):
                load(i * GROUP + q * n + k, width)
            return 0

        lax.fori_loop(0, GROUP // n, some, 0)

    def store_group(i, width, n):
        def some(q, _):
            for k in range(n):
                store(i * GROUP + q * n + k, k % 2, width)
            return 0

        lax.fori_loop(0, GROUP // n, some, 0)

    load_group(0, NARROW, 4)

    def pipeline(i, _):
        prod = product(i)
        before = jnp.where(i == 0, gn, i - 1)
        for k in range(GROUP):
            store(before * GROUP + k, k % 2, NARROW)
        p_ref[rows_of(i), :] = prod
        for k in range(GROUP):
            load((i + 1) * GROUP + k, NARROW)
        return 0

    lax.fori_loop(0, gn, pipeline, 0)
    store_group(jnp.maximum(gn - 1, 0), NARROW, 4)

    def wide(i, _):
        load_group(i, WIDE, 1)
        p_ref[rows_of(i), :] = product(i)
        store_group(i, WIDE, 1)
        return 0

    lax.fori_loop(gn + 1, gn + 1 + gw, wide, 0)

    def read(b):
        return acc0_ref[:, at(b + RB)] + acc1_ref[:, at(b + RB)]

    compress(read, z_ref, src_ref, start_ref)
    add_to_masters(z_ref, oh_ref, pe_ref, w_ref, g_ref, lhs_ref)
    hanging_values(z_ref, oh_ref, pe_ref, w_ref, g_ref, lhs_ref, hq_ref)
    new_ref = outs[0] if number < 3 else ext_ref

    def finish(i, _):
        for k in range(UNROLL):
            b = i * UNROLL + k
            t = expand(b, read(b), z_ref, posr_ref, start_ref)
            r = (t - CENTRE * u_ref[:, at(b)]) * ((1.0 if number == 1 else 2.0) / HALF)
            if number > 1:
                r = r - prev_ref[:, at(b)]
            new_ref[:, at(b)] = r
        return 0

    lax.fori_loop(0, NB // UNROLL, finish, 0)
    if number < 3:
        outs[1][...] = new_ref[:, 0:RIM]
        outs[2][...] = new_ref[:, LOC - RIM :]
    else:
        me = lax.axis_index("band")
        q = LOC // 4
        for k in range(4):
            outs[k][...] = new_ref[:, pl.ds(pl.multiple_of(((me + k) & 3) * q, L), q)]


def apply_step(number, u, gl, gr, prev, cell, base, hang, start):
    if number == 3:
        shapes = (sds((S, LOC // 4)),) * 4
    else:
        shapes = (sds((S, LOC)), sds((S, RIM)), sds((S, RIM)))
    return pl.pallas_call(
        functools.partial(step_kernel, number),
        out_shape=shapes,
        in_specs=[VM] * 14 + [SM] * 2,
        out_specs=(VM,) * len(shapes),
        scratch_shapes=[
            pltpu.VMEM((S, EXT), F32),
            pltpu.VMEM((S, EXT), F32),
            pltpu.VMEM((S, EXT), F32),
            pltpu.VMEM((RING * S, NPAD), F32),
            pltpu.VMEM((RING * S, NPAD), F32),
            *HANG_SCRATCH,
        ],
        compiler_params=pltpu.CompilerParams(vmem_limit_bytes=VLIM),
        name=f"step{number}",
    )(u, gl, gr, prev, *cell, *hang, base, start)


def gram_kernel(q0_ref, q1_ref, q2_ref, q3_ref, gram_ref, all_ref):
    me = lax.axis_index("band")
    for k, ref in enumerate((q0_ref, q1_ref, q2_ref, q3_ref)):
        all_ref[pl.ds(pl.multiple_of(((me - k) & 3) * S, S), S), :] = ref[...]
    a = all_ref[...]
    gram_ref[...] = lax.dot_general(a, a, NT, preferred_element_type=F32, precision=lax.Precision.HIGHEST)


def gram_of(qs):
    n = qs[0].shape[1]
    return pl.pallas_call(
        gram_kernel,
        out_shape=(sds((4 * S, 4 * S)), sds((4 * S, n))),
        in_specs=[VM] * 4,
        out_specs=(VM, VM),
        compiler_params=pltpu.CompilerParams(vmem_limit_bytes=VLIM),
        name="gram",
    )(*qs)


def basis_kernel(total, gram_ref, all_ref, o0_ref, o1_ref, o2_ref, o3_ref, m_ref, r_ref):
    n = 4 * S
    eye = (iota((n, n), 0) == iota((n, n), 1)).astype(F32)
    m_ref[...] = jnp.concatenate([gram_ref[...], eye], 1)
    row_id = iota((n, 2 * n), 0)

    m = m_ref[...]
    for j in range(n):
        pivot = m[j : j + 1, :]
        scaled = pivot * (1.0 / pivot[:, j : j + 1])
        m = m - jnp.where(row_id > j, m[:, j : j + 1], 0.0) * scaled
    dg = jnp.sum(jnp.where(row_id == iota((n, 2 * n), 1), m, 0.0), axis=1, keepdims=True)
    inv = m[:, n:] * lax.rsqrt(dg) * jnp.sqrt(jnp.float32(total))
    r_ref[...] = jnp.dot(inv, all_ref[...], preferred_element_type=F32, precision=lax.Precision.HIGHEST)
    me = lax.axis_index("band")
    for k, ref in enumerate((o0_ref, o1_ref, o2_ref, o3_ref)):
        ref[...] = r_ref[pl.ds(pl.multiple_of(((me + k) & 3) * S, S), S), :]


def basis_of(gram, rows, total):
    n = rows.shape[1]
    return pl.pallas_call(
        functools.partial(basis_kernel, total),
        out_shape=(sds((S, n)),) * 4,
        in_specs=[VM, VM],
        out_specs=(VM,) * 4,
        scratch_shapes=[pltpu.VMEM((4 * S, 8 * S), F32), pltpu.VMEM((4 * S, n), F32)],
        compiler_params=pltpu.CompilerParams(vmem_limit_bytes=VLIM),
        name="basis",
    )(gram, rows)


def join_kernel(q0_ref, q1_ref, q2_ref, q3_ref, out_ref):
    me = lax.axis_index("band")
    n = q0_ref.shape[1]
    for k, ref in enumerate((q0_ref, q1_ref, q2_ref, q3_ref)):
        out_ref[:, pl.ds(pl.multiple_of(((me - k) & 3) * n, L), n)] = ref[...]


def join(qs):
    return pl.pallas_call(
        join_kernel,
        out_shape=sds((S, LOC)),
        in_specs=[VM] * 4,
        out_specs=VM,
        compiler_params=pltpu.CompilerParams(vmem_limit_bytes=VLIM),
        name="join",
    )(*qs)


def shift(x, axis, by):
    size = lax.axis_size(axis)
    return lax.ppermute(x, axis, [(i, (i + by) % size) for i in range(size)])


def swap(x, axis, bits):
    size = lax.axis_size(axis)
    return lax.ppermute(x, axis, [(i, i ^ bits) for i in range(size)])


def summed(g):
    g = g + swap(g, "dom", 1)
    for axis, unit in (("dom", 2), ("dom", 8), ("band", 1)):
        others = [swap(g, axis, unit * k) for k in (1, 2, 3)]
        g = (g + others[0]) + (others[1] + others[2])
    return g


def body(
    block,
    stiffness,
    cell_scale,
    potential,
    cell_dofs,
    cell_count,
    hang_rows,
    hang_masters,
    hang_weights,
):
    own, hanging = pack(
        cell_dofs.T, potential.T, cell_scale, hang_rows, hang_masters, hang_weights, cell_count
    )
    from_left = shift(own, "dom", 1)
    from_right = shift(own, "dom", -1)
    *hang, start, u0, first, last = prepare(hanging, block)

    def ghosts(first, last):
        return shift(last, "dom", 1), shift(first, "dom", -1)

    gl, gr = ghosts(first, last)
    *cell, base = cell_tables(own, from_left, from_right, hang[0], stiffness)
    args = (cell, base, hang, start)
    u1, first, last = apply_step(1, u0, gl, gr, u0, *args)
    gl, gr = ghosts(first, last)
    u2, first, last = apply_step(2, u1, gl, gr, u0, *args)
    gl, gr = ghosts(first, last)
    qs = apply_step(3, u2, gl, gr, u1, *args)
    qs = [qs[0]] + [shift(qs[k], "band", k) for k in (1, 2, 3)]
    gram, rows = gram_of(qs)
    gram = summed(gram)
    outs = basis_of(gram, rows, LOC * lax.axis_size("dom"))
    outs = [outs[0]] + [shift(outs[k], "band", k) for k in (1, 2, 3)]
    return join(outs)


def solution(mesh):
    return jax.shard_map(
        body,
        mesh=mesh,
        in_specs=(
            P("band", "dom"),
            P(),
            P("dom"),
            P(None, "dom"),
            P(None, "dom"),
            P("dom"),
            P("dom"),
            P(None, "dom"),
            P(None, "dom"),
        ),
        out_specs=P("band", "dom"),
        check_vma=False,
    )
```

profile of v0, /device:TPU:0, one launch (start us, length us, event | category | flops | bytes accessed | tf_op | source)
XLA Modules:
  0.0 150.9 jit_solution(3204035062013287052)
XLA Ops:
  0.7 1.7 %pack.1 = (f32[72,896]{1,0:T(8,128)}, f32[9,896]{1,0:T(8,128)}) custom-call(s32[64,343]{1,0:T(8,128)} %bitcast.2, f32[64,343]{1,0:T(8,128)} %bitcast.3, f32[64]{0:T(128)} %scale_hbm.1, s32[864]{0:T(1024)} %rows_hbm.1, s32[4,864]{1,0:T(4,128)} %masters_hbm.1, f32[4,864]{1,0:T(4,128)} %weights_hbm.1, s32[1]{0:T(128)S(6)} %copy.10.count_ref), custom_call_target="tpu_custom_call" | custom-call | tf_op jit(solution)/shard_map/pack/pallas_call | solution.py:333
  2.4 4.8 %collective-permute-start.3 = (f32[72,896]{1,0:T(8,128)}, f32[72,896]{1,0:T(8,128)S(1)}, u32[]{:S(2)}, u32[]{:S(2)}) collective-permute-start(f32[72,896]{1,0:T(8,128)} %get-tuple-element.42.own_ref), channel_id=1, source_target_pairs={{0,124},{4,0},{8,4},{12,8},{16,12},{20,16},{24,20},{28,24},{32,28}... | collective-permute-start | bytes 774152 | tf_op jit(solution)/shard_map/ppermute | solution.py:721
  9.2 9.5 %prepare.1 = (s32[1,4608]{1,0:T(1,128)S(1)}, f32[1,3584]{1,0:T(1,128)S(1)}, s32[40,128]{1,0:T(8,128)S(1)}, s32[128,128]{1,0:T(8,128)S(1)}, f32[16,512]{1,0:T(8,1...) custom-call(f32[9,896]{1,0:T(8,128)S(1)} %copy-done.3, ...), custom_call_target="tpu_custom_call" | custom-call | tf_op jit(solution)/shard_map/prepare/pallas_call | solution.py:273
  18.8 5.1 %collective-permute-start.1 = (f32[16,2048]{1,0:T(8,128)S(1)}, f32[16,2048]{1,0:T(8,128)S(1)}, u32[]{:S(2)}, u32[]{:S(2)}) collective-permute-start(f32[16,2048]{1,0:T(8,128)S(1)} %get-tuple-element.41), channel_id=1, source_target_pairs={{0,124},{4,0},{8,4},{12,8},{16,12},{20,16},{24,20},{28,24},{32,28}... | collective-permute-start | bytes 393224 | tf_op jit(solution)/shard_map/ppermute | solution.py:721
  25.9 8.4 %cell_tables.1 = (s32[224,16,128]{2,1,0:T(8,128)S(1)}, f32[224,8,128]{2,1,0:T(8,128)S(1)}, bf16[384,384]{1,0:T(8,128)(2,1)S(1)}, bf16[384,384]{1,0:T(8,128)(2,1)...) custom-call(f32[72,896]{1,0:T(8,128)S(1)} %copy-done.2, f32[72,896]{1,0:T(8,128)S(1)} %collective-permute-done.2.left_ref, ...), custom_call_target="tpu_custom_call" | custom-call | tf_op jit(solution)/shard_map/cell_tables/pallas_call | solution.py:470
  34.3 15.6 %step1.1 = (f32[16,13824]{1,0:T(8,128)S(1)}, f32[16,2048]{1,0:T(8,128)S(1)}, f32[16,2048]{1,0:T(8,128)S(1)}) custom-call(f32[16,13824]{1,0:T(8,128)S(1)} %get-tuple-element.39.refs_0_.refs_3_, f32[16,2048]{1,0:T(8,128)S(1)} %collective-permute-done.refs_1_, f32[16,2048]{1,0:T(8,128)S(1)} %collective-permute-done.1.refs_2_, ...), custom_call_target="tpu_custom_call" | custom-call | tf_op jit(solution)/shard_map/step1/pallas_call | solution.py:631
  50.0 5.1 %collective-permute-start.5 = (f32[16,2048]{1,0:T(8,128)S(1)}, f32[16,2048]{1,0:T(8,128)S(1)}, u32[]{:S(2)}, u32[]{:S(2)}) collective-permute-start(f32[16,2048]{1,0:T(8,128)S(1)} %get-tuple-element.57), channel_id=1, source_target_pairs={{0,124},{4,0},{8,4},{12,8},{16,12},{20,16},{24,20},{28,24},{32,28}... | collective-permute-start | bytes 393224 | tf_op jit(solution)/shard_map/ppermute | solution.py:721
  55.0 2.6 %collective-permute-done.4.refs_1_ = f32[16,2048]{1,0:T(8,128)S(1)} collective-permute-done((f32[16,2048]{1,0:T(8,128)S(1)}, f32[16,2048]{1,0:T(8,128)S(1)}, u32[]{:S(2)}, u32[]{:S(2)}) %collective-permute-start.4) | collective-permute-done | bytes 131104 | tf_op jit(solution)/shard_map/ppermute | solution.py:721
  57.7 15.4 %step2.1 = (f32[16,13824]{1,0:T(8,128)S(1)}, f32[16,2048]{1,0:T(8,128)S(1)}, f32[16,2048]{1,0:T(8,128)S(1)}) custom-call(f32[16,13824]{1,0:T(8,128)S(1)} %get-tuple-element.55.refs_0_.refs_3_, f32[16,2048]{1,0:T(8,128)S(1)} %collective-permute-done.4.refs_1_, f32[16,2048]{1,0:T(8,128)S(1)} %collective-permute-done.5.refs_2_, ...), custom_call_target="tpu_custom_call" | custom-call | tf_op jit(solution)/shard_map/step2/pallas_call | solution.py:631
  73.2 5.1 %collective-permute-start.7 = (f32[16,2048]{1,0:T(8,128)S(1)}, f32[16,2048]{1,0:T(8,128)S(1)}, u32[]{:S(2)}, u32[]{:S(2)}) collective-permute-start(f32[16,2048]{1,0:T(8,128)S(1)} %get-tuple-element.60), channel_id=1, source_target_pairs={{0,124},{4,0},{8,4},{12,8},{16,12},{20,16},{24,20},{28,24},{32,28}... | collective-permute-start | bytes 393224 | tf_op jit(solution)/shard_map/ppermute | solution.py:721
  78.2 2.6 %collective-permute-done.6.refs_1_ = f32[16,2048]{1,0:T(8,128)S(1)} collective-permute-done((f32[16,2048]{1,0:T(8,128)S(1)}, f32[16,2048]{1,0:T(8,128)S(1)}, u32[]{:S(2)}, u32[]{:S(2)}) %collective-permute-start.6) | collective-permute-done | bytes 131104 | tf_op jit(solution)/shard_map/ppermute | solution.py:721
  80.9 15.7 %step3.1 = (f32[16,3456]{1,0:T(8,128)S(1)}, f32[16,3456]{1,0:T(8,128)S(1)}, f32[16,3456]{1,0:T(8,128)S(1)}, f32[16,3456]{1,0:T(8,128)S(1)}) custom-call(f32[16,13824]{1,0:T(8,128)S(1)} %get-tuple-element.58.refs_0_, f32[16,2048]{1,0:T(8,128)S(1)} %collective-permute-done.6.refs_1_, f32[16,2048]{1,0:T(8,128)S(1)} %collective-permute-done.7.refs_2_, ...), custom_call_target="tpu_custom_call" | custom-call | tf_op jit(solution)/shard_map/step3/pallas_call | solution.py:631
  96.6 2.0 %collective-permute-start.8 = (f32[16,3456]{1,0:T(8,128)S(1)}, f32[16,3456]{1,0:T(8,128)S(1)}, u32[]{:S(2)}, u32[]{:S(2)}) collective-permute-start(f32[16,3456]{1,0:T(8,128)S(1)} %get-tuple-element.62), channel_id=1, source_target_pairs={{0,1},{1,2},{2,3},{3,0},{4,5},{5,6},{6,7},{7,4},{8,9},{9,10},{10,1... | collective-permute-start | bytes 663560 | tf_op jit(solution)/shard_map/ppermute | solution.py:721
  98.6 3.6 %collective-permute-start.9 = (f32[16,3456]{1,0:T(8,128)S(1)}, f32[16,3456]{1,0:T(8,128)S(1)}, u32[]{:S(2)}, u32[]{:S(2)}) collective-permute-start(f32[16,3456]{1,0:T(8,128)S(1)} %get-tuple-element.63), channel_id=1, source_target_pairs={{0,2},{1,3},{2,0},{3,1},{4,6},{5,7},{6,4},{7,5},{8,10},{9,11},{10,... | collective-permute-start | bytes 663560 | tf_op jit(solution)/shard_map/ppermute | solution.py:721
  104.6 3.8 %collective-permute-done.9.q2_ref = f32[16,3456]{1,0:T(8,128)S(1)} collective-permute-done((f32[16,3456]{1,0:T(8,128)S(1)}, f32[16,3456]{1,0:T(8,128)S(1)}, u32[]{:S(2)}, u32[]{:S(2)}) %collective-permute-start.9) | collective-permute-done | bytes 221216 | tf_op jit(solution)/shard_map/ppermute | solution.py:721
  110.7 4.0 %collective-permute-start.12 = (f32[64,64]{1,0:T(8,128)S(1)}, f32[64,64]{1,0:T(8,128)S(1)}, u32[]{:S(2)}, u32[]{:S(2)}) collective-permute-start(f32[64,64]{1,0:T(8,128)S(1)} %add.30), channel_id=1, source_target_pairs={{0,8},{4,12},{8,0},{12,4},{16,24},{20,28},{24,16},{28,20},{32,40},... | collective-permute-start | bytes 49160 | tf_op jit(solution)/shard_map/ppermute | solution.py:726
  117.0 2.8 %collective-permute-start.17 = (f32[64,64]{1,0:T(8,128)S(1)}, f32[64,64]{1,0:T(8,128)S(1)}, u32[]{:S(2)}, u32[]{:S(2)}) collective-permute-start(f32[64,64]{1,0:T(8,128)S(1)} %add_add_fusion.2), channel_id=1, source_target_pairs={{0,96},{4,100},{8,104},{12,108},{16,112},{20,116},{24,120},{28,124... | collective-permute-start | bytes 49160 | tf_op jit(solution)/shard_map/ppermute | solution.py:726
  122.2 3.0 %collective-permute-done.16 = f32[64,64]{1,0:T(8,128)S(1)} collective-permute-done((f32[64,64]{1,0:T(8,128)S(1)}, f32[64,64]{1,0:T(8,128)S(1)}, u32[]{:S(2)}, u32[]{:S(2)}) %collective-permute-start.16) | collective-permute-done | bytes 16416 | tf_op jit(solution)/shard_map/ppermute | solution.py:726
  125.2 2.4 %collective-permute-start.20 = (f32[64,64]{1,0:T(8,128)S(1)}, f32[64,64]{1,0:T(8,128)S(1)}, u32[]{:S(2)}, u32[]{:S(2)}) collective-permute-start(f32[64,64]{1,0:T(8,128)S(1)} %add_add_fusion.1), channel_id=1, source_target_pairs={{0,3},{1,2},{2,1},{3,0},{4,7},{5,6},{6,5},{7,4},{8,11},{9,10},{10,... | collective-permute-start | bytes 49160 | tf_op jit(solution)/shard_map/ppermute | solution.py:726
  130.4 2.6 %collective-permute-done.19 = f32[64,64]{1,0:T(8,128)S(1)} collective-permute-done((f32[64,64]{1,0:T(8,128)S(1)}, f32[64,64]{1,0:T(8,128)S(1)}, u32[]{:S(2)}, u32[]{:S(2)}) %collective-permute-start.19) | collective-permute-done | bytes 16416 | tf_op jit(solution)/shard_map/ppermute | solution.py:726
  133.1 6.4 %basis.1 = (f32[16,3456]{1,0:T(8,128)S(1)}, f32[16,3456]{1,0:T(8,128)S(1)}, f32[16,3456]{1,0:T(8,128)S(1)}, f32[16,3456]{1,0:T(8,128)S(1)}) custom-call(f32[64,64]{1,0:T(8,128)S(1)} %add_add_fusion.gram_ref, f32[64,3456]{1,0:T(8,128)S(1)} %get-tuple-element.66.all_ref), custom_call_target="tpu_custom_call" | custom-call | tf_op jit(solution)/shard_map/basis/pallas_call | solution.py:690
  139.8 2.6 %collective-permute-start.22 = (f32[16,3456]{1,0:T(8,128)S(1)}, f32[16,3456]{1,0:T(8,128)S(1)}, u32[]{:S(2)}, u32[]{:S(2)}) collective-permute-start(f32[16,3456]{1,0:T(8,128)S(1)} %get-tuple-element.69), channel_id=1, source_target_pairs={{0,2},{1,3},{2,0},{3,1},{4,6},{5,7},{6,4},{7,5},{8,10},{9,11},{10,... | collective-permute-start | bytes 663560 | tf_op jit(solution)/shard_map/ppermute | solution.py:721
  142.4 1.8 %collective-permute-start.23 = (f32[16,3456]{1,0:T(8,128)S(1)}, f32[16,3456]{1,0:T(8,128)S(1)}, u32[]{:S(2)}, u32[]{:S(2)}) collective-permute-start(f32[16,3456]{1,0:T(8,128)S(1)} %get-tuple-element.70), channel_id=1, source_target_pairs={{0,3},{1,0},{2,1},{3,2},{4,7},{5,4},{6,5},{7,6},{8,11},{9,8},{10,9... | collective-permute-start | bytes 663560 | tf_op jit(solution)/shard_map/ppermute | solution.py:721
  144.2 4.9 %collective-permute-done.21.q1_ref = f32[16,3456]{1,0:T(8,128)S(1)} collective-permute-done((f32[16,3456]{1,0:T(8,128)S(1)}, f32[16,3456]{1,0:T(8,128)S(1)}, u32[]{:S(2)}, u32[]{:S(2)}) %collective-permute-start.21) | collective-permute-done | bytes 221216 | tf_op jit(solution)/shard_map/ppermute | solution.py:721
  (45 shorter events, 18.5 us)
Async XLA Ops:
  2.4 21.5 %collective-permute-start.3 = (f32[72,896]{1,0:T(8,128)}, f32[72,896]{1,0:T(8,128)S(1)}, u32[]{:S(2)}, u32[]{:S(2)}) collective-permute-start(f32[72,896]{1,0:T(8,128)} %get-tuple-element.42.own_ref), channel_id=1, source_target_pairs={{0,124},{4,0},{8,4},{12,8},{16,12},{20,16},{24,20},{28,24},{32,28}... | collective-permute-start | bytes 774152 | tf_op jit(solution)/shard_map/ppermute | solution.py:721
  7.2 16.7 %collective-permute-start.2 = (f32[72,896]{1,0:T(8,128)}, f32[72,896]{1,0:T(8,128)S(1)}, u32[]{:S(2)}, u32[]{:S(2)}) collective-permute-start(f32[72,896]{1,0:T(8,128)} %get-tuple-element.42.own_ref), channel_id=1, source_target_pairs={{0,4},{4,8},{8,12},{12,16},{16,20},{20,24},{24,28},{28,32},{32,36}... | collective-permute-start | bytes 774152 | tf_op jit(solution)/shard_map/ppermute | solution.py:721
  18.7 15.6 %collective-permute-start = (f32[16,2048]{1,0:T(8,128)S(1)}, f32[16,2048]{1,0:T(8,128)S(1)}, u32[]{:S(2)}, u32[]{:S(2)}) collective-permute-start(f32[16,2048]{1,0:T(8,128)S(1)} %get-tuple-element.40), channel_id=1, source_target_pairs={{0,4},{4,8},{8,12},{12,16},{16,20},{20,24},{24,28},{28,32},{32,36}... | collective-permute-start | bytes 393224 | tf_op jit(solution)/shard_map/ppermute | solution.py:721
  18.8 15.5 %collective-permute-start.1 = (f32[16,2048]{1,0:T(8,128)S(1)}, f32[16,2048]{1,0:T(8,128)S(1)}, u32[]{:S(2)}, u32[]{:S(2)}) collective-permute-start(f32[16,2048]{1,0:T(8,128)S(1)} %get-tuple-element.41), channel_id=1, source_target_pairs={{0,124},{4,0},{8,4},{12,8},{16,12},{20,16},{24,20},{28,24},{32,28}... | collective-permute-start | bytes 393224 | tf_op jit(solution)/shard_map/ppermute | solution.py:721
  49.9 7.8 %collective-permute-start.4 = (f32[16,2048]{1,0:T(8,128)S(1)}, f32[16,2048]{1,0:T(8,128)S(1)}, u32[]{:S(2)}, u32[]{:S(2)}) collective-permute-start(f32[16,2048]{1,0:T(8,128)S(1)} %get-tuple-element.56), channel_id=1, source_target_pairs={{0,4},{4,8},{8,12},{12,16},{16,20},{20,24},{24,28},{28,32},{32,36}... | collective-permute-start | bytes 393224 | tf_op jit(solution)/shard_map/ppermute | solution.py:721
  50.0 7.7 %collective-permute-start.5 = (f32[16,2048]{1,0:T(8,128)S(1)}, f32[16,2048]{1,0:T(8,128)S(1)}, u32[]{:S(2)}, u32[]{:S(2)}) collective-permute-start(f32[16,2048]{1,0:T(8,128)S(1)} %get-tuple-element.57), channel_id=1, source_target_pairs={{0,124},{4,0},{8,4},{12,8},{16,12},{20,16},{24,20},{28,24},{32,28}... | collective-permute-start | bytes 393224 | tf_op jit(solution)/shard_map/ppermute | solution.py:721
  73.1 7.8 %collective-permute-start.6 = (f32[16,2048]{1,0:T(8,128)S(1)}, f32[16,2048]{1,0:T(8,128)S(1)}, u32[]{:S(2)}, u32[]{:S(2)}) collective-permute-start(f32[16,2048]{1,0:T(8,128)S(1)} %get-tuple-element.59), channel_id=1, source_target_pairs={{0,4},{4,8},{8,12},{12,16},{16,20},{20,24},{24,28},{28,32},{32,36}... | collective-permute-start | bytes 393224 | tf_op jit(solution)/shard_map/ppermute | solution.py:721
  73.2 7.7 %collective-permute-start.7 = (f32[16,2048]{1,0:T(8,128)S(1)}, f32[16,2048]{1,0:T(8,128)S(1)}, u32[]{:S(2)}, u32[]{:S(2)}) collective-permute-start(f32[16,2048]{1,0:T(8,128)S(1)} %get-tuple-element.60), channel_id=1, source_target_pairs={{0,124},{4,0},{8,4},{12,8},{16,12},{20,16},{24,20},{28,24},{32,28}... | collective-permute-start | bytes 393224 | tf_op jit(solution)/shard_map/ppermute | solution.py:721
  96.6 8.0 %collective-permute-start.8 = (f32[16,3456]{1,0:T(8,128)S(1)}, f32[16,3456]{1,0:T(8,128)S(1)}, u32[]{:S(2)}, u32[]{:S(2)}) collective-permute-start(f32[16,3456]{1,0:T(8,128)S(1)} %get-tuple-element.62), channel_id=1, source_target_pairs={{0,1},{1,2},{2,3},{3,0},{4,5},{5,6},{6,7},{7,4},{8,9},{9,10},{10,1... | collective-permute-start | bytes 663560 | tf_op jit(solution)/shard_map/ppermute | solution.py:721
  98.6 9.9 %collective-permute-start.9 = (f32[16,3456]{1,0:T(8,128)S(1)}, f32[16,3456]{1,0:T(8,128)S(1)}, u32[]{:S(2)}, u32[]{:S(2)}) collective-permute-start(f32[16,3456]{1,0:T(8,128)S(1)} %get-tuple-element.63), channel_id=1, source_target_pairs={{0,2},{1,3},{2,0},{3,1},{4,6},{5,7},{6,4},{7,5},{8,10},{9,11},{10,... | collective-permute-start | bytes 663560 | tf_op jit(solution)/shard_map/ppermute | solution.py:721
  102.1 6.3 %collective-permute-start.10 = (f32[16,3456]{1,0:T(8,128)S(1)}, f32[16,3456]{1,0:T(8,128)S(1)}, u32[]{:S(2)}, u32[]{:S(2)}) collective-permute-start(f32[16,3456]{1,0:T(8,128)S(1)} %get-tuple-element.64), channel_id=1, source_target_pairs={{0,3},{1,0},{2,1},{3,2},{4,7},{5,4},{6,5},{7,6},{8,11},{9,8},{10,9... | collective-permute-start | bytes 663560 | tf_op jit(solution)/shard_map/ppermute | solution.py:721
  109.3 1.3 collective-permute-start.11
  110.6 5.1 %collective-permute-start.14 = (f32[64,64]{1,0:T(8,128)S(1)}, f32[64,64]{1,0:T(8,128)S(1)}, u32[]{:S(2)}, u32[]{:S(2)}) collective-permute-start(f32[64,64]{1,0:T(8,128)S(1)} %add.30), channel_id=1, source_target_pairs={{0,24},{4,28},{8,16},{12,20},{16,8},{20,12},{24,0},{28,4},{32,56},... | collective-permute-start | bytes 49160 | tf_op jit(solution)/shard_map/ppermute | solution.py:726
  110.6 5.8 %collective-permute-start.13 = (f32[64,64]{1,0:T(8,128)S(1)}, f32[64,64]{1,0:T(8,128)S(1)}, u32[]{:S(2)}, u32[]{:S(2)}) collective-permute-start(f32[64,64]{1,0:T(8,128)S(1)} %add.30), channel_id=1, source_target_pairs={{0,16},{4,20},{8,24},{12,28},{16,0},{20,4},{24,8},{28,12},{32,48},... | collective-permute-start | bytes 49160 | tf_op jit(solution)/shard_map/ppermute | solution.py:726
  110.7 6.2 %collective-permute-start.12 = (f32[64,64]{1,0:T(8,128)S(1)}, f32[64,64]{1,0:T(8,128)S(1)}, u32[]{:S(2)}, u32[]{:S(2)}) collective-permute-start(f32[64,64]{1,0:T(8,128)S(1)} %add.30), channel_id=1, source_target_pairs={{0,8},{4,12},{8,0},{12,4},{16,24},{20,28},{24,16},{28,20},{32,40},... | collective-permute-start | bytes 49160 | tf_op jit(solution)/shard_map/ppermute | solution.py:726
  117.0 5.2 %collective-permute-start.17 = (f32[64,64]{1,0:T(8,128)S(1)}, f32[64,64]{1,0:T(8,128)S(1)}, u32[]{:S(2)}, u32[]{:S(2)}) collective-permute-start(f32[64,64]{1,0:T(8,128)S(1)} %add_add_fusion.2), channel_id=1, source_target_pairs={{0,96},{4,100},{8,104},{12,108},{16,112},{20,116},{24,120},{28,124... | collective-permute-start | bytes 49160 | tf_op jit(solution)/shard_map/ppermute | solution.py:726
  119.8 5.4 %collective-permute-start.16 = (f32[64,64]{1,0:T(8,128)S(1)}, f32[64,64]{1,0:T(8,128)S(1)}, u32[]{:S(2)}, u32[]{:S(2)}) collective-permute-start(f32[64,64]{1,0:T(8,128)S(1)} %add_add_fusion.2), channel_id=1, source_target_pairs={{0,64},{4,68},{8,72},{12,76},{16,80},{20,84},{24,88},{28,92},{32,9... | collective-permute-start | bytes 49160 | tf_op jit(solution)/shard_map/ppermute | solution.py:726
  119.8 5.4 %collective-permute-start.15 = (f32[64,64]{1,0:T(8,128)S(1)}, f32[64,64]{1,0:T(8,128)S(1)}, u32[]{:S(2)}, u32[]{:S(2)}) collective-permute-start(f32[64,64]{1,0:T(8,128)S(1)} %add_add_fusion.2), channel_id=1, source_target_pairs={{0,32},{4,36},{8,40},{12,44},{16,48},{20,52},{24,56},{28,60},{32,0... | collective-permute-start | bytes 49160 | tf_op jit(solution)/shard_map/ppermute | solution.py:726
  125.2 5.2 %collective-permute-start.20 = (f32[64,64]{1,0:T(8,128)S(1)}, f32[64,64]{1,0:T(8,128)S(1)}, u32[]{:S(2)}, u32[]{:S(2)}) collective-permute-start(f32[64,64]{1,0:T(8,128)S(1)} %add_add_fusion.1), channel_id=1, source_target_pairs={{0,3},{1,2},{2,1},{3,0},{4,7},{5,6},{6,5},{7,4},{8,11},{9,10},{10,... | collective-permute-start | bytes 49160 | tf_op jit(solution)/shard_map/ppermute | solution.py:726
  127.6 5.4 %collective-permute-start.19 = (f32[64,64]{1,0:T(8,128)S(1)}, f32[64,64]{1,0:T(8,128)S(1)}, u32[]{:S(2)}, u32[]{:S(2)}) collective-permute-start(f32[64,64]{1,0:T(8,128)S(1)} %add_add_fusion.1), channel_id=1, source_target_pairs={{0,2},{1,3},{2,0},{3,1},{4,6},{5,7},{6,4},{7,5},{8,10},{9,11},{10,... | collective-permute-start | bytes 49160 | tf_op jit(solution)/shard_map/ppermute | solution.py:726
  128.9 4.2 %collective-permute-start.18 = (f32[64,64]{1,0:T(8,128)S(1)}, f32[64,64]{1,0:T(8,128)S(1)}, u32[]{:S(2)}, u32[]{:S(2)}) collective-permute-start(f32[64,64]{1,0:T(8,128)S(1)} %add_add_fusion.1), channel_id=1, source_target_pairs={{0,1},{1,0},{2,3},{3,2},{4,5},{5,4},{6,7},{7,6},{8,9},{9,8},{10,11... | collective-permute-start | bytes 49160 | tf_op jit(solution)/shard_map/ppermute | solution.py:726
  139.5 9.6 %collective-permute-start.21 = (f32[16,3456]{1,0:T(8,128)S(1)}, f32[16,3456]{1,0:T(8,128)S(1)}, u32[]{:S(2)}, u32[]{:S(2)}) collective-permute-start(f32[16,3456]{1,0:T(8,128)S(1)} %get-tuple-element.68), channel_id=1, source_target_pairs={{0,1},{1,2},{2,3},{3,0},{4,5},{5,6},{6,7},{7,4},{8,9},{9,10},{10,1... | collective-permute-start | bytes 663560 | tf_op jit(solution)/shard_map/ppermute | solution.py:721
  139.8 9.3 %collective-permute-start.22 = (f32[16,3456]{1,0:T(8,128)S(1)}, f32[16,3456]{1,0:T(8,128)S(1)}, u32[]{:S(2)}, u32[]{:S(2)}) collective-permute-start(f32[16,3456]{1,0:T(8,128)S(1)} %get-tuple-element.69), channel_id=1, source_target_pairs={{0,2},{1,3},{2,0},{3,1},{4,6},{5,7},{6,4},{7,5},{8,10},{9,11},{10,... | collective-permute-start | bytes 663560 | tf_op jit(solution)/shard_map/ppermute | solution.py:721
  142.4 7.5 %collective-permute-start.23 = (f32[16,3456]{1,0:T(8,128)S(1)}, f32[16,3456]{1,0:T(8,128)S(1)}, u32[]{:S(2)}, u32[]{:S(2)}) collective-permute-start(f32[16,3456]{1,0:T(8,128)S(1)} %get-tuple-element.70), channel_id=1, source_target_pairs={{0,3},{1,0},{2,1},{3,2},{4,7},{5,4},{6,5},{7,6},{8,11},{9,8},{10,9... | collective-permute-start | bytes 663560 | tf_op jit(solution)/shard_map/ppermute | solution.py:721
  (4 other events, 4.0 us)
where the time goes:
time: 151 us
  Pallas kernels  74.5 us (49%)
  starting transfers between devices  44.1 us (29%)
  waiting for transfers between devices  27.5 us (18%)
  local copies, waits for them, and re-layouts  3.98 us (3%)
    pallas_call x3, Pallas kernels, apply_step(): pl.pallas_call(functools.partial(step_kernel, number), out_shape=shapes,...  46.7 us
    ppermute x14, starting transfers between devices, shift(): return lax.ppermute(x, axis, [(i, (i + by) % size) for i in range(size)])  31.6 us
    ppermute x14, waiting for transfers between devices, shift(): return lax.ppermute(x, axis, [(i, (i + by) % size) for i in range(size)])  16.3 us
    ppermute x10, starting transfers between devices, swap(): return lax.ppermute(x, axis, [(i, i ^ bits) for i in range(size)])  12.5 us
    ppermute x10, waiting for transfers between devices, swap(): return lax.ppermute(x, axis, [(i, i ^ bits) for i in range(size)])  11.2 us
    pallas_call x1, Pallas kernels, prepare(): pl.pallas_call(prepare_kernel, out_shape=(sds((1, E), I32), sds((1, ME)),...  9.51 us
    pallas_call x1, Pallas kernels, cell_tables(): pl.pallas_call(cells_kernel, out_shape=(sds((SLOTS, 16, L), I32), sds((SL...  8.39 us
    pallas_call x1, Pallas kernels, basis_of(): pl.pallas_call(functools.partial(basis_kernel, total), out_shape=(sds((S,...  6.38 us
  transfers between devices with their start and end apart: 24, of which 14 were waited for; matrix products, arithmetic and copies ran while one was open for 0% of the time, Pallas kernels for 12%

commit v1 on v0

--- a/solution.py
+++ b/solution.py
@@ -23,9 +23,8 @@
 NARROW = 3
 PACK = 72
 PW = 2 * NPAD + L
-GROUP = 16
-RING = 4 * GROUP
-SLOTS = 14 * GROUP
+GROUP = 8
+SLOTS = 28 * GROUP
 HPAD = 896
 HB = HPAD // L
 ME = MASTERS * HPAD
@@ -406,7 +405,7 @@
     pad_ref[...] = jnp.zeros_like(pad_ref)
     load.wait()
     pad_ref[0:NODES, 0:NODES] = k_ref[...]
-    kh_ref[...], kl_ref[...] = split(pad_ref[...])
+    kh_ref[...], kl_ref[...] = split(pad_ref[...].T)
     for i in range(E // L):
         col = slice(i * L, (i + 1) * L)
         oh_ref[:, col] = one_hot(pe_ref[0:1, col] & (QLO - 1), QLO).astype(BF16)
@@ -420,7 +419,7 @@
         return n + jnp.where(kind == 0, 1, 0), m + jnp.where(kind == 1, 1, 0)
 
     n, m = lax.fori_loop(0, 3 * CELLS, scan, (0, 0), unroll=4)
-    gn = (n + GROUP - 1) // GROUP
+    gn = 2 * ((n + 2 * GROUP - 1) // (2 * GROUP))
     gw = (m + GROUP - 1) // GROUP
     first = (gn + 1) * GROUP
     last = first + gw * GROUP
@@ -499,7 +498,7 @@
     (u_ref, gl_ref, gr_ref, prev_ref, tab_ref, pot_ref, kh_ref, kl_ref,
      oh_ref, pe_ref, w_ref, src_ref, posr_ref, hq_ref, base_ref, start_ref) = refs[:16]
     outs = refs[16 : 16 + (4 if number == 3 else 3)]
-    ext_ref, acc0_ref, acc1_ref, x_ref, p_ref, z_ref, g_ref, lhs_ref = refs[16 + len(outs) :]
+    ext_ref, acc0_ref, acc1_ref, x0_ref, x1_ref, p0_ref, p1_ref, z_ref, g_ref, lhs_ref = refs[16 + len(outs) :]
     accs = (acc0_ref, acc1_ref)
     ext_ref[:, 0:RIM] = jnp.where(inside(0), gl_ref[...], 0.0)
     ext_ref[:, RIM : RIM + LOC] = u_ref[...]
@@ -509,7 +508,11 @@
     gn = base_ref[4 * SLOTS]
     gw = base_ref[4 * SLOTS + 1]
 
-    def load(slot, width):
+    def rows8(k, s):
+        return pl.ds(k * S + 8 * s, 8) if isinstance(k, int) else pl.ds(pl.multiple_of(k * S + 8 * s, 8), 8)
+
+    def load(x_ref, group, k, width):
+        slot = group * GROUP + k
         for j in range(NJ):
             b = base_ref[4 * slot + j]
             row = jnp.broadcast_to(tab_ref[slot, j : j + 1, :], (8, L))
@@ -519,11 +522,11 @@
                 acc = lanes(ext_ref[r, at(b)], lo)
                 for t in range(1, width):
                     acc = jnp.where(hi == t, lanes(ext_ref[r, at(b + t)], lo), acc)
-                x_ref[pl.ds(pl.multiple_of((slot & (RING - 1)) * S + 8 * s, 8), 8), j * L : (j + 1) * L] = acc
-
-    def store(slot, parity, width):
-        acc_ref = accs[parity]
-        scale = jnp.broadcast_to(pot_ref[slot, 3:4, :], (8, L))
+                x_ref[rows8(k, s), j * L : (j + 1) * L] = acc
+
+    def store(p_ref, group, k, width):
+        slot = group * GROUP + k
+        acc_ref = accs[k % 2 if isinstance(k, int) else 0]
         if width == NARROW:
             inv = [[tab_ref[slot, 3 + 3 * j + t : 4 + 3 * j + t, :] for t in range(width)] for j in range(NJ)]
         else:
@@ -531,12 +534,7 @@
             inv = [[full[8 * j + t : 8 * j + t + 1] for t in range(width)] for j in range(NJ)]
         for j in range(NJ):
             b = base_ref[4 * slot + j]
-            col = slice(j * L, (j + 1) * L)
-            pot = jnp.broadcast_to(pot_ref[slot, j : j + 1, :], (8, L))
-            vals = []
-            for s in range(2):
-                r = pl.ds(pl.multiple_of((slot & (RING - 1)) * S + 8 * s, 8), 8)
-                vals.append(scale * p_ref[r, col] + pot * x_ref[r, col])
+            vals = [p_ref[rows8(k, s), j * L : (j + 1) * L] for s in range(2)]
             adds = []
             for t in range(width):
                 row = jnp.broadcast_to(inv[j][t], (8, L))
@@ -547,49 +545,57 @@
                 for s in range(2):
                     acc_ref[8 * s : 8 * s + 8, at(b + t)] = olds[t][s] + adds[t][s]
 
-    def rows_of(i):
-        return pl.ds(pl.multiple_of((i & 3) * (GROUP * S), GROUP * S), GROUP * S)
-
-    def product(i):
-        xh, xl = split(x_ref[rows_of(i), :])
-        kh, kl = kh_ref[...], kl_ref[...]
-        return nt(xh, kh) + (nt(xl, kh) + nt(xh, kl))
-
-    def load_group(i, width, n):
+    def product(x_ref, p_ref, group):
+        n = GROUP * S
+        x = x_ref[...]
+        xh, xl = split(x)
+        both = nn(jnp.concatenate([xh, xl], 0), kh_ref[...])
+        prod = both[:n] + (both[n:] + nn(xh, kl_ref[...]))
+        for k in range(GROUP):
+            slot = group * GROUP + k
+            r = slice(k * S, (k + 1) * S)
+            scale = jnp.broadcast_to(pot_ref[slot, 3:4, :], (S, L))
+            for j in range(NJ):
+                col = slice(j * L, (j + 1) * L)
+                pot = jnp.broadcast_to(pot_ref[slot, j : j + 1, :], (S, L))
+                p_ref[r, col] = scale * prod[r, col] + pot * x[r, col]
+
+    def load_group(x_ref, group, width, n):
         def some(q, _):
             for k in range(n):
-                load(i * GROUP + q * n + k, width)
+                load(x_ref, group, q * n + k, width)
             return 0
 
         lax.fori_loop(0, GROUP // n, some, 0)
 
-    def store_group(i, width, n):
-        def some(q, _):
-            for k in range(n):
-                store(i * GROUP + q * n + k, k % 2, width)
+    load_group(x0_ref, 0, NARROW, 4)
+
+    def pipeline(i, _):
+        g = 2 * i
+        product(x0_ref, p0_ref, g)
+        before = jnp.where(i == 0, gn, g - 1)
+        for k in range(GROUP):
+            store(p1_ref, before, k, NARROW)
+            load(x1_ref, g + 1, k, NARROW)
+        product(x1_ref, p1_ref, g + 1)
+        for k in range(GROUP):
+            store(p0_ref, g, k, NARROW)
+            load(x0_ref, g + 2, k, NARROW)
+        return 0
+
+    lax.fori_loop(0, gn // 2, pipeline, 0)
+    for k in range(GROUP):
+        store(p1_ref, jnp.where(gn > 0, gn - 1, gn), k, NARROW)
+
+    def wide(i, _):
+        load_group(x0_ref, i, WIDE, 1)
+        product(x0_ref, p0_ref, i)
+
+        def one(k, _):
+            store(p0_ref, i, k, WIDE)
             return 0
 
-        lax.fori_loop(0, GROUP // n, some, 0)
-
-    load_group(0, NARROW, 4)
-
-    def pipeline(i, _):
-        prod = product(i)
-        before = jnp.where(i == 0, gn, i - 1)
-        for k in range(GROUP):
-            store(before * GROUP + k, k % 2, NARROW)
-        p_ref[rows_of(i), :] = prod
-        for k in range(GROUP):
-            load((i + 1) * GROUP + k, NARROW)
-        return 0
-
-    lax.fori_loop(0, gn, pipeline, 0)
-    store_group(jnp.maximum(gn - 1, 0), NARROW, 4)
-
-    def wide(i, _):
-        load_group(i, WIDE, 1)
-        p_ref[rows_of(i), :] = product(i)
-        store_group(i, WIDE, 1)
+        lax.fori_loop(0, GROUP, one, 0)
         return 0
 
     lax.fori_loop(gn + 1, gn + 1 + gw, wide, 0)
@@ -637,8 +643,7 @@
             pltpu.VMEM((S, EXT), F32),
             pltpu.VMEM((S, EXT), F32),
             pltpu.VMEM((S, EXT), F32),
-            pltpu.VMEM((RING * S, NPAD), F32),
-            pltpu.VMEM((RING * S, NPAD), F32),
+            *[pltpu.VMEM((GROUP * S, NPAD), F32)] * 4,
             *HANG_SCRATCH,
         ],
         compiler_params=pltpu.CompilerParams(vmem_limit_bytes=VLIM),

time: 151 us -> 149 us (0.987)
  Pallas kernels: 74.5 us -> 71.8 us
    pallas_call x3, Pallas kernels: 46.7 us -> 44.4 us  [apply_step(): pl.pallas_call(functools.partial(step_kernel, number), out_shape=shapes,...]
where the time goes in v1:
time: 149 us; the launch traced here: 150 us
  Pallas kernels  71.8 us (48%)
  starting transfers between devices  45.1 us (30%)
  waiting for transfers between devices  27.8 us (19%)
  local copies, waits for them, and re-layouts  3.98 us (3%)
    pallas_call x3, Pallas kernels, apply_step(): pl.pallas_call(functools.partial(step_kernel, number), out_shape=shapes,...  44.4 us
    ppermute x14, starting transfers between devices, shift(): return lax.ppermute(x, axis, [(i, (i + by) % size) for i in range(size)])  31.6 us
    ppermute x14, waiting for transfers between devices, shift(): return lax.ppermute(x, axis, [(i, (i + by) % size) for i in range(size)])  16.2 us
    ppermute x10, starting transfers between devices, swap(): return lax.ppermute(x, axis, [(i, i ^ bits) for i in range(size)])  13.5 us
    ppermute x10, waiting for transfers between devices, swap(): return lax.ppermute(x, axis, [(i, i ^ bits) for i in range(size)])  11.6 us
    pallas_call x1, Pallas kernels, prepare(): pl.pallas_call(prepare_kernel, out_shape=(sds((1, E), I32), sds((1, ME)),...  9.51 us
    pallas_call x1, Pallas kernels, cell_tables(): pl.pallas_call(cells_kernel, out_shape=(sds((SLOTS, 16, L), I32), sds((SL...  7.98 us
    pallas_call x1, Pallas kernels, basis_of(): pl.pallas_call(functools.partial(basis_kernel, total), out_shape=(sds((S,...  6.38 us
  transfers between devices with their start and end apart: 24, of which 14 were waited for; matrix products, arithmetic and copies ran while one was open for 0% of the time, Pallas kernels for 12%

profile of v1, /device:TPU:0, one launch (start us, length us, event | category | flops | bytes accessed | tf_op | source)
XLA Modules:
  0.0 149.5 jit_solution(4263740258328497465)
XLA Ops:
  0.7 1.7 %pack.1 = (f32[72,896]{1,0:T(8,128)}, f32[9,896]{1,0:T(8,128)}) custom-call(s32[64,343]{1,0:T(8,128)} %bitcast.2, f32[64,343]{1,0:T(8,128)} %bitcast.3, f32[64]{0:T(128)} %scale_hbm.1, s32[864]{0:T(1024)} %rows_hbm.1, s32[4,864]{1,0:T(4,128)} %masters_hbm.1, f32[4,864]{1,0:T(4,128)} %weights_hbm.1, s32[1]{0:T(128)S(6)} %copy.10.count_ref), custom_call_target="tpu_custom_call" | custom-call | tf_op jit(solution)/shard_map/pack/pallas_call | solution.py:332
  2.4 4.8 %collective-permute-start.3 = (f32[72,896]{1,0:T(8,128)}, f32[72,896]{1,0:T(8,128)S(1)}, u32[]{:S(2)}, u32[]{:S(2)}) collective-permute-start(f32[72,896]{1,0:T(8,128)} %get-tuple-element.42.own_ref), channel_id=1, source_target_pairs={{0,124},{4,0},{8,4},{12,8},{16,12},{20,16},{24,20},{28,24},{32,28}... | collective-permute-start | bytes 774152 | tf_op jit(solution)/shard_map/ppermute | solution.py:726
  9.2 9.5 %prepare.1 = (s32[1,4608]{1,0:T(1,128)S(1)}, f32[1,3584]{1,0:T(1,128)S(1)}, s32[40,128]{1,0:T(8,128)S(1)}, s32[128,128]{1,0:T(8,128)S(1)}, f32[16,512]{1,0:T(8,1...) custom-call(f32[9,896]{1,0:T(8,128)S(1)} %copy-done.3, ...), custom_call_target="tpu_custom_call" | custom-call | tf_op jit(solution)/shard_map/prepare/pallas_call | solution.py:272
  18.8 5.1 %collective-permute-start.1 = (f32[16,2048]{1,0:T(8,128)S(1)}, f32[16,2048]{1,0:T(8,128)S(1)}, u32[]{:S(2)}, u32[]{:S(2)}) collective-permute-start(f32[16,2048]{1,0:T(8,128)S(1)} %get-tuple-element.41), channel_id=1, source_target_pairs={{0,124},{4,0},{8,4},{12,8},{16,12},{20,16},{24,20},{28,24},{32,28}... | collective-permute-start | bytes 393224 | tf_op jit(solution)/shard_map/ppermute | solution.py:726
  25.9 8.0 %cell_tables.1 = (s32[224,16,128]{2,1,0:T(8,128)S(1)}, f32[224,8,128]{2,1,0:T(8,128)S(1)}, bf16[384,384]{1,0:T(8,128)(2,1)S(1)}, bf16[384,384]{1,0:T(8,128)(2,1)...) custom-call(f32[72,896]{1,0:T(8,128)S(1)} %copy-done.2, f32[72,896]{1,0:T(8,128)S(1)} %collective-permute-done.2.left_ref, ...), custom_call_target="tpu_custom_call" | custom-call | tf_op jit(solution)/shard_map/cell_tables/pallas_call | solution.py:469
  33.9 14.8 %step1.1 = (f32[16,13824]{1,0:T(8,128)S(1)}, f32[16,2048]{1,0:T(8,128)S(1)}, f32[16,2048]{1,0:T(8,128)S(1)}) custom-call(f32[16,13824]{1,0:T(8,128)S(1)} %get-tuple-element.39.refs_0_.refs_3_, f32[16,2048]{1,0:T(8,128)S(1)} %collective-permute-done.refs_1_, f32[16,2048]{1,0:T(8,128)S(1)} %collective-permute-done.1.refs_2_, ...), custom_call_target="tpu_custom_call" | custom-call | tf_op jit(solution)/shard_map/step1/pallas_call | solution.py:637
  48.8 5.1 %collective-permute-start.5 = (f32[16,2048]{1,0:T(8,128)S(1)}, f32[16,2048]{1,0:T(8,128)S(1)}, u32[]{:S(2)}, u32[]{:S(2)}) collective-permute-start(f32[16,2048]{1,0:T(8,128)S(1)} %get-tuple-element.57), channel_id=1, source_target_pairs={{0,124},{4,0},{8,4},{12,8},{16,12},{20,16},{24,20},{28,24},{32,28}... | collective-permute-start | bytes 393224 | tf_op jit(solution)/shard_map/ppermute | solution.py:726
  53.9 2.6 %collective-permute-done.4.refs_1_ = f32[16,2048]{1,0:T(8,128)S(1)} collective-permute-done((f32[16,2048]{1,0:T(8,128)S(1)}, f32[16,2048]{1,0:T(8,128)S(1)}, u32[]{:S(2)}, u32[]{:S(2)}) %collective-permute-start.4) | collective-permute-done | bytes 131104 | tf_op jit(solution)/shard_map/ppermute | solution.py:726
  56.5 14.6 %step2.1 = (f32[16,13824]{1,0:T(8,128)S(1)}, f32[16,2048]{1,0:T(8,128)S(1)}, f32[16,2048]{1,0:T(8,128)S(1)}) custom-call(f32[16,13824]{1,0:T(8,128)S(1)} %get-tuple-element.55.refs_0_.refs_3_, f32[16,2048]{1,0:T(8,128)S(1)} %collective-permute-done.4.refs_1_, f32[16,2048]{1,0:T(8,128)S(1)} %collective-permute-done.5.refs_2_, ...), custom_call_target="tpu_custom_call" | custom-call | tf_op jit(solution)/shard_map/step2/pallas_call | solution.py:637
  71.2 5.1 %collective-permute-start.7 = (f32[16,2048]{1,0:T(8,128)S(1)}, f32[16,2048]{1,0:T(8,128)S(1)}, u32[]{:S(2)}, u32[]{:S(2)}) collective-permute-start(f32[16,2048]{1,0:T(8,128)S(1)} %get-tuple-element.60), channel_id=1, source_target_pairs={{0,124},{4,0},{8,4},{12,8},{16,12},{20,16},{24,20},{28,24},{32,28}... | collective-permute-start | bytes 393224 | tf_op jit(solution)/shard_map/ppermute | solution.py:726
  76.4 2.6 %collective-permute-done.6.refs_1_ = f32[16,2048]{1,0:T(8,128)S(1)} collective-permute-done((f32[16,2048]{1,0:T(8,128)S(1)}, f32[16,2048]{1,0:T(8,128)S(1)}, u32[]{:S(2)}, u32[]{:S(2)}) %collective-permute-start.6) | collective-permute-done | bytes 131104 | tf_op jit(solution)/shard_map/ppermute | solution.py:726
  79.0 14.9 %step3.1 = (f32[16,3456]{1,0:T(8,128)S(1)}, f32[16,3456]{1,0:T(8,128)S(1)}, f32[16,3456]{1,0:T(8,128)S(1)}, f32[16,3456]{1,0:T(8,128)S(1)}) custom-call(f32[16,13824]{1,0:T(8,128)S(1)} %get-tuple-element.58.refs_0_, f32[16,2048]{1,0:T(8,128)S(1)} %collective-permute-done.6.refs_1_, f32[16,2048]{1,0:T(8,128)S(1)} %collective-permute-done.7.refs_2_, ...), custom_call_target="tpu_custom_call" | custom-call | tf_op jit(solution)/shard_map/step3/pallas_call | solution.py:637
  93.9 2.0 %collective-permute-start.8 = (f32[16,3456]{1,0:T(8,128)S(1)}, f32[16,3456]{1,0:T(8,128)S(1)}, u32[]{:S(2)}, u32[]{:S(2)}) collective-permute-start(f32[16,3456]{1,0:T(8,128)S(1)} %get-tuple-element.62), channel_id=1, source_target_pairs={{0,1},{1,2},{2,3},{3,0},{4,5},{5,6},{6,7},{7,4},{8,9},{9,10},{10,1... | collective-permute-start | bytes 663560 | tf_op jit(solution)/shard_map/ppermute | solution.py:726
  95.9 3.6 %collective-permute-start.9 = (f32[16,3456]{1,0:T(8,128)S(1)}, f32[16,3456]{1,0:T(8,128)S(1)}, u32[]{:S(2)}, u32[]{:S(2)}) collective-permute-start(f32[16,3456]{1,0:T(8,128)S(1)} %get-tuple-element.63), channel_id=1, source_target_pairs={{0,2},{1,3},{2,0},{3,1},{4,6},{5,7},{6,4},{7,5},{8,10},{9,11},{10,... | collective-permute-start | bytes 663560 | tf_op jit(solution)/shard_map/ppermute | solution.py:726
  101.9 3.8 %collective-permute-done.9.q2_ref = f32[16,3456]{1,0:T(8,128)S(1)} collective-permute-done((f32[16,3456]{1,0:T(8,128)S(1)}, f32[16,3456]{1,0:T(8,128)S(1)}, u32[]{:S(2)}, u32[]{:S(2)}) %collective-permute-start.9) | collective-permute-done | bytes 221216 | tf_op jit(solution)/shard_map/ppermute | solution.py:726
  108.0 4.0 %collective-permute-start.12 = (f32[64,64]{1,0:T(8,128)S(1)}, f32[64,64]{1,0:T(8,128)S(1)}, u32[]{:S(2)}, u32[]{:S(2)}) collective-permute-start(f32[64,64]{1,0:T(8,128)S(1)} %add.30), channel_id=1, source_target_pairs={{0,8},{4,12},{8,0},{12,4},{16,24},{20,28},{24,16},{28,20},{32,40},... | collective-permute-start | bytes 49160 | tf_op jit(solution)/shard_map/ppermute | solution.py:731
  114.2 4.2 %collective-permute-start.17 = (f32[64,64]{1,0:T(8,128)S(1)}, f32[64,64]{1,0:T(8,128)S(1)}, u32[]{:S(2)}, u32[]{:S(2)}) collective-permute-start(f32[64,64]{1,0:T(8,128)S(1)} %add_add_fusion.2), channel_id=1, source_target_pairs={{0,96},{4,100},{8,104},{12,108},{16,112},{20,116},{24,120},{28,124... | collective-permute-start | bytes 49160 | tf_op jit(solution)/shard_map/ppermute | solution.py:731
  120.3 3.5 %collective-permute-done.16 = f32[64,64]{1,0:T(8,128)S(1)} collective-permute-done((f32[64,64]{1,0:T(8,128)S(1)}, f32[64,64]{1,0:T(8,128)S(1)}, u32[]{:S(2)}, u32[]{:S(2)}) %collective-permute-start.16) | collective-permute-done | bytes 16416 | tf_op jit(solution)/shard_map/ppermute | solution.py:731
  123.9 2.4 %collective-permute-start.20 = (f32[64,64]{1,0:T(8,128)S(1)}, f32[64,64]{1,0:T(8,128)S(1)}, u32[]{:S(2)}, u32[]{:S(2)}) collective-permute-start(f32[64,64]{1,0:T(8,128)S(1)} %add_add_fusion.1), channel_id=1, source_target_pairs={{0,3},{1,2},{2,1},{3,0},{4,7},{5,6},{6,5},{7,4},{8,11},{9,10},{10,... | collective-permute-start | bytes 49160 | tf_op jit(solution)/shard_map/ppermute | solution.py:731
  129.1 2.6 %collective-permute-done.19 = f32[64,64]{1,0:T(8,128)S(1)} collective-permute-done((f32[64,64]{1,0:T(8,128)S(1)}, f32[64,64]{1,0:T(8,128)S(1)}, u32[]{:S(2)}, u32[]{:S(2)}) %collective-permute-start.19) | collective-permute-done | bytes 16416 | tf_op jit(solution)/shard_map/ppermute | solution.py:731
  131.7 6.4 %basis.1 = (f32[16,3456]{1,0:T(8,128)S(1)}, f32[16,3456]{1,0:T(8,128)S(1)}, f32[16,3456]{1,0:T(8,128)S(1)}, f32[16,3456]{1,0:T(8,128)S(1)}) custom-call(f32[64,64]{1,0:T(8,128)S(1)} %add_add_fusion.gram_ref, f32[64,3456]{1,0:T(8,128)S(1)} %get-tuple-element.66.all_ref), custom_call_target="tpu_custom_call" | custom-call | tf_op jit(solution)/shard_map/basis/pallas_call | solution.py:695
  138.4 2.6 %collective-permute-start.22 = (f32[16,3456]{1,0:T(8,128)S(1)}, f32[16,3456]{1,0:T(8,128)S(1)}, u32[]{:S(2)}, u32[]{:S(2)}) collective-permute-start(f32[16,3456]{1,0:T(8,128)S(1)} %get-tuple-element.69), channel_id=1, source_target_pairs={{0,2},{1,3},{2,0},{3,1},{4,6},{5,7},{6,4},{7,5},{8,10},{9,11},{10,... | collective-permute-start | bytes 663560 | tf_op jit(solution)/shard_map/ppermute | solution.py:726
  141.0 1.8 %collective-permute-start.23 = (f32[16,3456]{1,0:T(8,128)S(1)}, f32[16,3456]{1,0:T(8,128)S(1)}, u32[]{:S(2)}, u32[]{:S(2)}) collective-permute-start(f32[16,3456]{1,0:T(8,128)S(1)} %get-tuple-element.70), channel_id=1, source_target_pairs={{0,3},{1,0},{2,1},{3,2},{4,7},{5,4},{6,5},{7,6},{8,11},{9,8},{10,9... | collective-permute-start | bytes 663560 | tf_op jit(solution)/shard_map/ppermute | solution.py:726
  142.8 4.9 %collective-permute-done.21.q1_ref = f32[16,3456]{1,0:T(8,128)S(1)} collective-permute-done((f32[16,3456]{1,0:T(8,128)S(1)}, f32[16,3456]{1,0:T(8,128)S(1)}, u32[]{:S(2)}, u32[]{:S(2)}) %collective-permute-start.21) | collective-permute-done | bytes 221216 | tf_op jit(solution)/shard_map/ppermute | solution.py:726
  (45 shorter events, 18.1 us)
Async XLA Ops:
  2.4 21.5 %collective-permute-start.3 = (f32[72,896]{1,0:T(8,128)}, f32[72,896]{1,0:T(8,128)S(1)}, u32[]{:S(2)}, u32[]{:S(2)}) collective-permute-start(f32[72,896]{1,0:T(8,128)} %get-tuple-element.42.own_ref), channel_id=1, source_target_pairs={{0,124},{4,0},{8,4},{12,8},{16,12},{20,16},{24,20},{28,24},{32,28}... | collective-permute-start | bytes 774152 | tf_op jit(solution)/shard_map/ppermute | solution.py:726
  7.2 16.7 %collective-permute-start.2 = (f32[72,896]{1,0:T(8,128)}, f32[72,896]{1,0:T(8,128)S(1)}, u32[]{:S(2)}, u32[]{:S(2)}) collective-permute-start(f32[72,896]{1,0:T(8,128)} %get-tuple-element.42.own_ref), channel_id=1, source_target_pairs={{0,4},{4,8},{8,12},{12,16},{16,20},{20,24},{24,28},{28,32},{32,36}... | collective-permute-start | bytes 774152 | tf_op jit(solution)/shard_map/ppermute | solution.py:726
  18.7 15.2 %collective-permute-start = (f32[16,2048]{1,0:T(8,128)S(1)}, f32[16,2048]{1,0:T(8,128)S(1)}, u32[]{:S(2)}, u32[]{:S(2)}) collective-permute-start(f32[16,2048]{1,0:T(8,128)S(1)} %get-tuple-element.40), channel_id=1, source_target_pairs={{0,4},{4,8},{8,12},{12,16},{16,20},{20,24},{24,28},{28,32},{32,36}... | collective-permute-start | bytes 393224 | tf_op jit(solution)/shard_map/ppermute | solution.py:726
  18.8 15.1 %collective-permute-start.1 = (f32[16,2048]{1,0:T(8,128)S(1)}, f32[16,2048]{1,0:T(8,128)S(1)}, u32[]{:S(2)}, u32[]{:S(2)}) collective-permute-start(f32[16,2048]{1,0:T(8,128)S(1)} %get-tuple-element.41), channel_id=1, source_target_pairs={{0,124},{4,0},{8,4},{12,8},{16,12},{20,16},{24,20},{28,24},{32,28}... | collective-permute-start | bytes 393224 | tf_op jit(solution)/shard_map/ppermute | solution.py:726
  48.7 7.8 %collective-permute-start.4 = (f32[16,2048]{1,0:T(8,128)S(1)}, f32[16,2048]{1,0:T(8,128)S(1)}, u32[]{:S(2)}, u32[]{:S(2)}) collective-permute-start(f32[16,2048]{1,0:T(8,128)S(1)} %get-tuple-element.56), channel_id=1, source_target_pairs={{0,4},{4,8},{8,12},{12,16},{16,20},{20,24},{24,28},{28,32},{32,36}... | collective-permute-start | bytes 393224 | tf_op jit(solution)/shard_map/ppermute | solution.py:726
  48.8 7.7 %collective-permute-start.5 = (f32[16,2048]{1,0:T(8,128)S(1)}, f32[16,2048]{1,0:T(8,128)S(1)}, u32[]{:S(2)}, u32[]{:S(2)}) collective-permute-start(f32[16,2048]{1,0:T(8,128)S(1)} %get-tuple-element.57), channel_id=1, source_target_pairs={{0,124},{4,0},{8,4},{12,8},{16,12},{20,16},{24,20},{28,24},{32,28}... | collective-permute-start | bytes 393224 | tf_op jit(solution)/shard_map/ppermute | solution.py:726
  71.2 7.8 %collective-permute-start.6 = (f32[16,2048]{1,0:T(8,128)S(1)}, f32[16,2048]{1,0:T(8,128)S(1)}, u32[]{:S(2)}, u32[]{:S(2)}) collective-permute-start(f32[16,2048]{1,0:T(8,128)S(1)} %get-tuple-element.59), channel_id=1, source_target_pairs={{0,4},{4,8},{8,12},{12,16},{16,20},{20,24},{24,28},{28,32},{32,36}... | collective-permute-start | bytes 393224 | tf_op jit(solution)/shard_map/ppermute | solution.py:726
  71.2 7.7 %collective-permute-start.7 = (f32[16,2048]{1,0:T(8,128)S(1)}, f32[16,2048]{1,0:T(8,128)S(1)}, u32[]{:S(2)}, u32[]{:S(2)}) collective-permute-start(f32[16,2048]{1,0:T(8,128)S(1)} %get-tuple-element.60), channel_id=1, source_target_pairs={{0,124},{4,0},{8,4},{12,8},{16,12},{20,16},{24,20},{28,24},{32,28}... | collective-permute-start | bytes 393224 | tf_op jit(solution)/shard_map/ppermute | solution.py:726
  93.9 8.0 %collective-permute-start.8 = (f32[16,3456]{1,0:T(8,128)S(1)}, f32[16,3456]{1,0:T(8,128)S(1)}, u32[]{:S(2)}, u32[]{:S(2)}) collective-permute-start(f32[16,3456]{1,0:T(8,128)S(1)} %get-tuple-element.62), channel_id=1, source_target_pairs={{0,1},{1,2},{2,3},{3,0},{4,5},{5,6},{6,7},{7,4},{8,9},{9,10},{10,1... | collective-permute-start | bytes 663560 | tf_op jit(solution)/shard_map/ppermute | solution.py:726
  95.9 9.9 %collective-permute-start.9 = (f32[16,3456]{1,0:T(8,128)S(1)}, f32[16,3456]{1,0:T(8,128)S(1)}, u32[]{:S(2)}, u32[]{:S(2)}) collective-permute-start(f32[16,3456]{1,0:T(8,128)S(1)} %get-tuple-element.63), channel_id=1, source_target_pairs={{0,2},{1,3},{2,0},{3,1},{4,6},{5,7},{6,4},{7,5},{8,10},{9,11},{10,... | collective-permute-start | bytes 663560 | tf_op jit(solution)/shard_map/ppermute | solution.py:726
  99.4 6.3 %collective-permute-start.10 = (f32[16,3456]{1,0:T(8,128)S(1)}, f32[16,3456]{1,0:T(8,128)S(1)}, u32[]{:S(2)}, u32[]{:S(2)}) collective-permute-start(f32[16,3456]{1,0:T(8,128)S(1)} %get-tuple-element.64), channel_id=1, source_target_pairs={{0,3},{1,0},{2,1},{3,2},{4,7},{5,4},{6,5},{7,6},{8,11},{9,8},{10,9... | collective-permute-start | bytes 663560 | tf_op jit(solution)/shard_map/ppermute | solution.py:726
  106.6 1.3 collective-permute-start.11
  107.9 5.1 %collective-permute-start.14 = (f32[64,64]{1,0:T(8,128)S(1)}, f32[64,64]{1,0:T(8,128)S(1)}, u32[]{:S(2)}, u32[]{:S(2)}) collective-permute-start(f32[64,64]{1,0:T(8,128)S(1)} %add.30), channel_id=1, source_target_pairs={{0,24},{4,28},{8,16},{12,20},{16,8},{20,12},{24,0},{28,4},{32,56},... | collective-permute-start | bytes 49160 | tf_op jit(solution)/shard_map/ppermute | solution.py:731
  107.9 5.8 %collective-permute-start.13 = (f32[64,64]{1,0:T(8,128)S(1)}, f32[64,64]{1,0:T(8,128)S(1)}, u32[]{:S(2)}, u32[]{:S(2)}) collective-permute-start(f32[64,64]{1,0:T(8,128)S(1)} %add.30), channel_id=1, source_target_pairs={{0,16},{4,20},{8,24},{12,28},{16,0},{20,4},{24,8},{28,12},{32,48},... | collective-permute-start | bytes 49160 | tf_op jit(solution)/shard_map/ppermute | solution.py:731
  108.0 6.2 %collective-permute-start.12 = (f32[64,64]{1,0:T(8,128)S(1)}, f32[64,64]{1,0:T(8,128)S(1)}, u32[]{:S(2)}, u32[]{:S(2)}) collective-permute-start(f32[64,64]{1,0:T(8,128)S(1)} %add.30), channel_id=1, source_target_pairs={{0,8},{4,12},{8,0},{12,4},{16,24},{20,28},{24,16},{28,20},{32,40},... | collective-permute-start | bytes 49160 | tf_op jit(solution)/shard_map/ppermute | solution.py:731
  114.2 6.1 %collective-permute-start.17 = (f32[64,64]{1,0:T(8,128)S(1)}, f32[64,64]{1,0:T(8,128)S(1)}, u32[]{:S(2)}, u32[]{:S(2)}) collective-permute-start(f32[64,64]{1,0:T(8,128)S(1)} %add_add_fusion.2), channel_id=1, source_target_pairs={{0,96},{4,100},{8,104},{12,108},{16,112},{20,116},{24,120},{28,124... | collective-permute-start | bytes 49160 | tf_op jit(solution)/shard_map/ppermute | solution.py:731
  118.5 5.4 %collective-permute-start.16 = (f32[64,64]{1,0:T(8,128)S(1)}, f32[64,64]{1,0:T(8,128)S(1)}, u32[]{:S(2)}, u32[]{:S(2)}) collective-permute-start(f32[64,64]{1,0:T(8,128)S(1)} %add_add_fusion.2), channel_id=1, source_target_pairs={{0,64},{4,68},{8,72},{12,76},{16,80},{20,84},{24,88},{28,92},{32,9... | collective-permute-start | bytes 49160 | tf_op jit(solution)/shard_map/ppermute | solution.py:731
  118.5 5.4 %collective-permute-start.15 = (f32[64,64]{1,0:T(8,128)S(1)}, f32[64,64]{1,0:T(8,128)S(1)}, u32[]{:S(2)}, u32[]{:S(2)}) collective-permute-start(f32[64,64]{1,0:T(8,128)S(1)} %add_add_fusion.2), channel_id=1, source_target_pairs={{0,32},{4,36},{8,40},{12,44},{16,48},{20,52},{24,56},{28,60},{32,0... | collective-permute-start | bytes 49160 | tf_op jit(solution)/shard_map/ppermute | solution.py:731
  123.9 5.2 %collective-permute-start.20 = (f32[64,64]{1,0:T(8,128)S(1)}, f32[64,64]{1,0:T(8,128)S(1)}, u32[]{:S(2)}, u32[]{:S(2)}) collective-permute-start(f32[64,64]{1,0:T(8,128)S(1)} %add_add_fusion.1), channel_id=1, source_target_pairs={{0,3},{1,2},{2,1},{3,0},{4,7},{5,6},{6,5},{7,4},{8,11},{9,10},{10,... | collective-permute-start | bytes 49160 | tf_op jit(solution)/shard_map/ppermute | solution.py:731
  126.3 5.4 %collective-permute-start.19 = (f32[64,64]{1,0:T(8,128)S(1)}, f32[64,64]{1,0:T(8,128)S(1)}, u32[]{:S(2)}, u32[]{:S(2)}) collective-permute-start(f32[64,64]{1,0:T(8,128)S(1)} %add_add_fusion.1), channel_id=1, source_target_pairs={{0,2},{1,3},{2,0},{3,1},{4,6},{5,7},{6,4},{7,5},{8,10},{9,11},{10,... | collective-permute-start | bytes 49160 | tf_op jit(solution)/shard_map/ppermute | solution.py:731
  127.5 4.2 %collective-permute-start.18 = (f32[64,64]{1,0:T(8,128)S(1)}, f32[64,64]{1,0:T(8,128)S(1)}, u32[]{:S(2)}, u32[]{:S(2)}) collective-permute-start(f32[64,64]{1,0:T(8,128)S(1)} %add_add_fusion.1), channel_id=1, source_target_pairs={{0,1},{1,0},{2,3},{3,2},{4,5},{5,4},{6,7},{7,6},{8,9},{9,8},{10,11... | collective-permute-start | bytes 49160 | tf_op jit(solution)/shard_map/ppermute | solution.py:731
  138.1 9.6 %collective-permute-start.21 = (f32[16,3456]{1,0:T(8,128)S(1)}, f32[16,3456]{1,0:T(8,128)S(1)}, u32[]{:S(2)}, u32[]{:S(2)}) collective-permute-start(f32[16,3456]{1,0:T(8,128)S(1)} %get-tuple-element.68), channel_id=1, source_target_pairs={{0,1},{1,2},{2,3},{3,0},{4,5},{5,6},{6,7},{7,4},{8,9},{9,10},{10,1... | collective-permute-start | bytes 663560 | tf_op jit(solution)/shard_map/ppermute | solution.py:726
  138.4 9.3 %collective-permute-start.22 = (f32[16,3456]{1,0:T(8,128)S(1)}, f32[16,3456]{1,0:T(8,128)S(1)}, u32[]{:S(2)}, u32[]{:S(2)}) collective-permute-start(f32[16,3456]{1,0:T(8,128)S(1)} %get-tuple-element.69), channel_id=1, source_target_pairs={{0,2},{1,3},{2,0},{3,1},{4,6},{5,7},{6,4},{7,5},{8,10},{9,11},{10,... | collective-permute-start | bytes 663560 | tf_op jit(solution)/shard_map/ppermute | solution.py:726
  141.0 7.5 %collective-permute-start.23 = (f32[16,3456]{1,0:T(8,128)S(1)}, f32[16,3456]{1,0:T(8,128)S(1)}, u32[]{:S(2)}, u32[]{:S(2)}) collective-permute-start(f32[16,3456]{1,0:T(8,128)S(1)} %get-tuple-element.70), channel_id=1, source_target_pairs={{0,3},{1,0},{2,1},{3,2},{4,7},{5,4},{6,5},{7,6},{8,11},{9,8},{10,9... | collective-permute-start | bytes 663560 | tf_op jit(solution)/shard_map/ppermute | solution.py:726
  (4 other events, 4.0 us)

commit v2 on v1

--- a/solution.py
+++ b/solution.py
@@ -7,6 +7,7 @@
 from jax.sharding import PartitionSpec as P
 
 RIM = 2048
+EDGE = 768
 NODES = 343
 HANG = 864
 MASTERS = 4
@@ -77,6 +78,10 @@
 
 def at(b):
     return pl.ds(pl.multiple_of(b * L, L), L)
+
+
+def blocks(b, n):
+    return pl.ds(pl.multiple_of(b * L, L), n * L)
 
 
 def one_hot(row, n):
@@ -253,8 +258,8 @@
         return 0
 
     lax.fori_loop(0, NB // UNROLL, step, 0)
-    left_ref[...] = u_ref[:, 0:RIM]
-    right_ref[...] = u_ref[:, LOC - RIM :]
+    left_ref[...] = u_ref[:, 0:EDGE]
+    right_ref[...] = u_ref[:, LOC - EDGE :]
 
 
 def sds(shape, dtype=F32):
@@ -279,8 +284,8 @@
             sds((16, QLO)),
             sds((8, L), I32),
             sds((S, LOC)),
-            sds((S, RIM)),
-            sds((S, RIM)),
+            sds((S, EDGE)),
+            sds((S, EDGE)),
         ),
         in_specs=[VM] * 2,
         out_specs=(VM,) * 9,
@@ -500,9 +505,11 @@
     outs = refs[16 : 16 + (4 if number == 3 else 3)]
     ext_ref, acc0_ref, acc1_ref, x0_ref, x1_ref, p0_ref, p1_ref, z_ref, g_ref, lhs_ref = refs[16 + len(outs) :]
     accs = (acc0_ref, acc1_ref)
-    ext_ref[:, 0:RIM] = jnp.where(inside(0), gl_ref[...], 0.0)
+    ext_ref[:, 0 : RIM - EDGE] = jnp.zeros((S, RIM - EDGE), F32)
+    ext_ref[:, RIM + LOC + EDGE :] = jnp.zeros((S, RIM - EDGE), F32)
+    ext_ref[:, RIM - EDGE : RIM] = jnp.where(inside(0), gl_ref[...], 0.0)
     ext_ref[:, RIM : RIM + LOC] = u_ref[...]
-    ext_ref[:, RIM + LOC :] = jnp.where(inside(1), gr_ref[...], 0.0)
+    ext_ref[:, RIM + LOC : RIM + LOC + EDGE] = jnp.where(inside(1), gr_ref[...], 0.0)
     for ref in accs:
         ref[...] = jnp.zeros_like(ref)
     gn = base_ref[4 * SLOTS]
@@ -519,9 +526,10 @@
             lo, hi = row & 127, row >> 7
             for s in range(2):
                 r = slice(8 * s, 8 * s + 8)
-                acc = lanes(ext_ref[r, at(b)], lo)
+                rows = ext_ref[r, blocks(b, width)]
+                acc = lanes(rows[:, 0:L], lo)
                 for t in range(1, width):
-                    acc = jnp.where(hi == t, lanes(ext_ref[r, at(b + t)], lo), acc)
+                    acc = jnp.where(hi == t, lanes(rows[:, t * L : (t + 1) * L], lo), acc)
                 x_ref[rows8(k, s), j * L : (j + 1) * L] = acc
 
     def store(p_ref, group, k, width):
@@ -540,10 +548,9 @@
                 row = jnp.broadcast_to(inv[j][t], (8, L))
                 m, lo = row >= 0, row & 127
                 adds.append([jnp.where(m, lanes(vals[s], lo), 0.0) for s in range(2)])
-            olds = [[acc_ref[8 * s : 8 * s + 8, at(b + t)] for s in range(2)] for t in range(width)]
-            for t in range(width):
-                for s in range(2):
-                    acc_ref[8 * s : 8 * s + 8, at(b + t)] = olds[t][s] + adds[t][s]
+            for s in range(2):
+                more = jnp.concatenate([adds[t][s] for t in range(width)], axis=1)
+                acc_ref[8 * s : 8 * s + 8, blocks(b, width)] += more
 
     def product(x_ref, p_ref, group):
         n = GROUP * S
@@ -620,8 +627,8 @@
 
     lax.fori_loop(0, NB // UNROLL, finish, 0)
     if number < 3:
-        outs[1][...] = new_ref[:, 0:RIM]
-        outs[2][...] = new_ref[:, LOC - RIM :]
+        outs[1][...] = new_ref[:, 0:EDGE]
+        outs[2][...] = new_ref[:, LOC - EDGE :]
     else:
         me = lax.axis_index("band")
         q = LOC // 4
@@ -633,7 +640,7 @@
     if number == 3:
         shapes = (sds((S, LOC // 4)),) * 4
     else:
-        shapes = (sds((S, LOC)), sds((S, RIM)), sds((S, RIM)))
+        shapes = (sds((S, LOC)), sds((S, EDGE)), sds((S, EDGE)))
     return pl.pallas_call(
         functools.partial(step_kernel, number),
         out_shape=shapes,

time: 149 us -> 143 us (0.960)
  Pallas kernels: 71.8 us -> 66.5 us
  waiting for transfers between devices: 27.8 us -> 26.1 us
    pallas_call x3, Pallas kernels: 44.4 us -> 39.9 us  [apply_step(): pl.pallas_call(functools.partial(step_kernel, number), out_shape=shapes,...]
    ppermute x14, waiting for transfers between devices: 16.2 us -> 14.5 us  [shift(): return lax.ppermute(x, axis, [(i, (i + by) % size) for i in range(size)])]
  transfers between devices with their start and end apart: 24 -> 24, of which waited for: 14 -> 15; matrix products, arithmetic and copies ran while one was open for 0% -> 0% of each run, Pallas kernels for 12% -> 12%
where the time goes in v2:
time: 143 us
  Pallas kernels  66.5 us (47%)
  starting transfers between devices  45.8 us (32%)
  waiting for transfers between devices  26.1 us (18%)
  local copies, waits for them, and re-layouts  3.98 us (3%)
    pallas_call x3, Pallas kernels, apply_step(): pl.pallas_call(functools.partial(step_kernel, number), out_shape=shapes,...  39.9 us
    ppermute x14, starting transfers between devices, shift(): return lax.ppermute(x, axis, [(i, (i + by) % size) for i in range(size)])  31.6 us
    ppermute x14, waiting for transfers between devices, shift(): return lax.ppermute(x, axis, [(i, (i + by) % size) for i in range(size)])  14.5 us
    ppermute x10, starting transfers between devices, swap(): return lax.ppermute(x, axis, [(i, i ^ bits) for i in range(size)])  14.1 us
    ppermute x10, waiting for transfers between devices, swap(): return lax.ppermute(x, axis, [(i, i ^ bits) for i in range(size)])  11.6 us
    pallas_call x1, Pallas kernels, prepare(): pl.pallas_call(prepare_kernel, out_shape=(sds((1, E), I32), sds((1, ME)),...  9.5 us
    pallas_call x1, Pallas kernels, cell_tables(): pl.pallas_call(cells_kernel, out_shape=(sds((SLOTS, 16, L), I32), sds((SL...  7.15 us
    pallas_call x1, Pallas kernels, basis_of(): pl.pallas_call(functools.partial(basis_kernel, total), out_shape=(sds((S,...  6.38 us
  transfers between devices with their start and end apart: 24, of which 15 were waited for; matrix products, arithmetic and copies ran while one was open for 0% of the time, Pallas kernels for 12%

profile of v2, /device:TPU:0, one launch (start us, length us, event | category | flops | bytes accessed | tf_op | source)
XLA Modules:
  0.0 143.1 jit_solution(3914229687804399818)
XLA Ops:
  0.7 1.7 %pack.1 = (f32[72,896]{1,0:T(8,128)}, f32[9,896]{1,0:T(8,128)}) custom-call(s32[64,343]{1,0:T(8,128)} %bitcast.2, f32[64,343]{1,0:T(8,128)} %bitcast.3, f32[64]{0:T(128)} %scale_hbm.1, s32[864]{0:T(1024)} %rows_hbm.1, s32[4,864]{1,0:T(4,128)} %masters_hbm.1, f32[4,864]{1,0:T(4,128)} %weights_hbm.1, s32[1]{0:T(128)S(6)} %copy.10.count_ref), custom_call_target="tpu_custom_call" | custom-call | tf_op jit(solution)/shard_map/pack/pallas_call | solution.py:337
  2.4 4.8 %collective-permute-start.3 = (f32[72,896]{1,0:T(8,128)}, f32[72,896]{1,0:T(8,128)S(1)}, u32[]{:S(2)}, u32[]{:S(2)}) collective-permute-start(f32[72,896]{1,0:T(8,128)} %get-tuple-element.42.own_ref), channel_id=1, source_target_pairs={{0,124},{4,0},{8,4},{12,8},{16,12},{20,16},{24,20},{28,24},{32,28}... | collective-permute-start | bytes 774152 | tf_op jit(solution)/shard_map/ppermute | solution.py:733
  9.2 9.5 %prepare.1 = (s32[1,4608]{1,0:T(1,128)S(1)}, f32[1,3584]{1,0:T(1,128)S(1)}, s32[40,128]{1,0:T(8,128)S(1)}, s32[128,128]{1,0:T(8,128)S(1)}, f32[16,512]{1,0:T(8,1...) custom-call(f32[9,896]{1,0:T(8,128)S(1)} %copy-done.3, ...), custom_call_target="tpu_custom_call" | custom-call | tf_op jit(solution)/shard_map/prepare/pallas_call | solution.py:277
  18.8 5.1 %collective-permute-start.1 = (f32[16,768]{1,0:T(8,128)S(1)}, f32[16,768]{1,0:T(8,128)S(1)}, u32[]{:S(2)}, u32[]{:S(2)}) collective-permute-start(f32[16,768]{1,0:T(8,128)S(1)} %get-tuple-element.41), channel_id=1, source_target_pairs={{0,124},{4,0},{8,4},{12,8},{16,12},{20,16},{24,20},{28,24},{32,28}... | collective-permute-start | bytes 147464 | tf_op jit(solution)/shard_map/ppermute | solution.py:733
  25.9 7.1 %cell_tables.1 = (s32[224,16,128]{2,1,0:T(8,128)S(1)}, f32[224,8,128]{2,1,0:T(8,128)S(1)}, bf16[384,384]{1,0:T(8,128)(2,1)S(1)}, bf16[384,384]{1,0:T(8,128)(2,1)...) custom-call(f32[72,896]{1,0:T(8,128)S(1)} %copy-done.2, f32[72,896]{1,0:T(8,128)S(1)} %collective-permute-done.2.left_ref, ...), custom_call_target="tpu_custom_call" | custom-call | tf_op jit(solution)/shard_map/cell_tables/pallas_call | solution.py:474
  33.1 13.3 %step1.1 = (f32[16,13824]{1,0:T(8,128)S(1)}, f32[16,768]{1,0:T(8,128)S(1)}, f32[16,768]{1,0:T(8,128)S(1)}) custom-call(f32[16,13824]{1,0:T(8,128)S(1)} %get-tuple-element.39.refs_0_.refs_3_, f32[16,768]{1,0:T(8,128)S(1)} %collective-permute-done.refs_1_, f32[16,768]{1,0:T(8,128)S(1)} %collective-permute-done.1.refs_2_, ...), custom_call_target="tpu_custom_call" | custom-call | tf_op jit(solution)/shard_map/step1/pallas_call | solution.py:644
  46.5 5.1 %collective-permute-start.5 = (f32[16,768]{1,0:T(8,128)S(1)}, f32[16,768]{1,0:T(8,128)S(1)}, u32[]{:S(2)}, u32[]{:S(2)}) collective-permute-start(f32[16,768]{1,0:T(8,128)S(1)} %get-tuple-element.57), channel_id=1, source_target_pairs={{0,124},{4,0},{8,4},{12,8},{16,12},{20,16},{24,20},{28,24},{32,28}... | collective-permute-start | bytes 147464 | tf_op jit(solution)/shard_map/ppermute | solution.py:733
  51.5 1.8 %collective-permute-done.4.refs_1_ = f32[16,768]{1,0:T(8,128)S(1)} collective-permute-done((f32[16,768]{1,0:T(8,128)S(1)}, f32[16,768]{1,0:T(8,128)S(1)}, u32[]{:S(2)}, u32[]{:S(2)}) %collective-permute-start.4) | collective-permute-done | bytes 49184 | tf_op jit(solution)/shard_map/ppermute | solution.py:733
  53.3 13.2 %step2.1 = (f32[16,13824]{1,0:T(8,128)S(1)}, f32[16,768]{1,0:T(8,128)S(1)}, f32[16,768]{1,0:T(8,128)S(1)}) custom-call(f32[16,13824]{1,0:T(8,128)S(1)} %get-tuple-element.55.refs_0_.refs_3_, f32[16,768]{1,0:T(8,128)S(1)} %collective-permute-done.4.refs_1_, f32[16,768]{1,0:T(8,128)S(1)} %collective-permute-done.5.refs_2_, ...), custom_call_target="tpu_custom_call" | custom-call | tf_op jit(solution)/shard_map/step2/pallas_call | solution.py:644
  66.5 5.1 %collective-permute-start.7 = (f32[16,768]{1,0:T(8,128)S(1)}, f32[16,768]{1,0:T(8,128)S(1)}, u32[]{:S(2)}, u32[]{:S(2)}) collective-permute-start(f32[16,768]{1,0:T(8,128)S(1)} %get-tuple-element.60), channel_id=1, source_target_pairs={{0,124},{4,0},{8,4},{12,8},{16,12},{20,16},{24,20},{28,24},{32,28}... | collective-permute-start | bytes 147464 | tf_op jit(solution)/shard_map/ppermute | solution.py:733
  73.4 13.4 %step3.1 = (f32[16,3456]{1,0:T(8,128)S(1)}, f32[16,3456]{1,0:T(8,128)S(1)}, f32[16,3456]{1,0:T(8,128)S(1)}, f32[16,3456]{1,0:T(8,128)S(1)}) custom-call(f32[16,13824]{1,0:T(8,128)S(1)} %get-tuple-element.58.refs_0_, f32[16,768]{1,0:T(8,128)S(1)} %collective-permute-done.6.refs_1_, f32[16,768]{1,0:T(8,128)S(1)} %collective-permute-done.7.refs_2_, ...), custom_call_target="tpu_custom_call" | custom-call | tf_op jit(solution)/shard_map/step3/pallas_call | solution.py:644
  86.8 2.0 %collective-permute-start.8 = (f32[16,3456]{1,0:T(8,128)S(1)}, f32[16,3456]{1,0:T(8,128)S(1)}, u32[]{:S(2)}, u32[]{:S(2)}) collective-permute-start(f32[16,3456]{1,0:T(8,128)S(1)} %get-tuple-element.62), channel_id=1, source_target_pairs={{0,1},{1,2},{2,3},{3,0},{4,5},{5,6},{6,7},{7,4},{8,9},{9,10},{10,1... | collective-permute-start | bytes 663560 | tf_op jit(solution)/shard_map/ppermute | solution.py:733
  88.8 3.6 %collective-permute-start.9 = (f32[16,3456]{1,0:T(8,128)S(1)}, f32[16,3456]{1,0:T(8,128)S(1)}, u32[]{:S(2)}, u32[]{:S(2)}) collective-permute-start(f32[16,3456]{1,0:T(8,128)S(1)} %get-tuple-element.63), channel_id=1, source_target_pairs={{0,2},{1,3},{2,0},{3,1},{4,6},{5,7},{6,4},{7,5},{8,10},{9,11},{10,... | collective-permute-start | bytes 663560 | tf_op jit(solution)/shard_map/ppermute | solution.py:733
  93.4 2.6 %collective-permute-done.8.q1_ref = f32[16,3456]{1,0:T(8,128)S(1)} collective-permute-done((f32[16,3456]{1,0:T(8,128)S(1)}, f32[16,3456]{1,0:T(8,128)S(1)}, u32[]{:S(2)}, u32[]{:S(2)}) %collective-permute-start.8) | collective-permute-done | bytes 221216 | tf_op jit(solution)/shard_map/ppermute | solution.py:733
  96.0 2.7 %collective-permute-done.9.q2_ref = f32[16,3456]{1,0:T(8,128)S(1)} collective-permute-done((f32[16,3456]{1,0:T(8,128)S(1)}, f32[16,3456]{1,0:T(8,128)S(1)}, u32[]{:S(2)}, u32[]{:S(2)}) %collective-permute-start.9) | collective-permute-done | bytes 221216 | tf_op jit(solution)/shard_map/ppermute | solution.py:733
  100.9 4.8 %collective-permute-start.14 = (f32[64,64]{1,0:T(8,128)S(1)}, f32[64,64]{1,0:T(8,128)S(1)}, u32[]{:S(2)}, u32[]{:S(2)}) collective-permute-start(f32[64,64]{1,0:T(8,128)S(1)} %add.30), channel_id=1, source_target_pairs={{0,24},{4,28},{8,16},{12,20},{16,8},{20,12},{24,0},{28,4},{32,56},... | collective-permute-start | bytes 49160 | tf_op jit(solution)/shard_map/ppermute | solution.py:738
  107.5 3.5 %collective-permute-done.13 = f32[64,64]{1,0:T(8,128)S(1)} collective-permute-done((f32[64,64]{1,0:T(8,128)S(1)}, f32[64,64]{1,0:T(8,128)S(1)}, u32[]{:S(2)}, u32[]{:S(2)}) %collective-permute-start.13) | collective-permute-done | bytes 16416 | tf_op jit(solution)/shard_map/ppermute | solution.py:738
  113.1 2.2 %collective-permute-start.15 = (f32[64,64]{1,0:T(8,128)S(1)}, f32[64,64]{1,0:T(8,128)S(1)}, u32[]{:S(2)}, u32[]{:S(2)}) collective-permute-start(f32[64,64]{1,0:T(8,128)S(1)} %add_add_fusion.2), channel_id=1, source_target_pairs={{0,32},{4,36},{8,40},{12,44},{16,48},{20,52},{24,56},{28,60},{32,0... | collective-permute-start | bytes 49160 | tf_op jit(solution)/shard_map/ppermute | solution.py:738
  117.5 2.4 %collective-permute-start.20 = (f32[64,64]{1,0:T(8,128)S(1)}, f32[64,64]{1,0:T(8,128)S(1)}, u32[]{:S(2)}, u32[]{:S(2)}) collective-permute-start(f32[64,64]{1,0:T(8,128)S(1)} %add_add_fusion.1), channel_id=1, source_target_pairs={{0,3},{1,2},{2,1},{3,0},{4,7},{5,6},{6,5},{7,4},{8,11},{9,10},{10,... | collective-permute-start | bytes 49160 | tf_op jit(solution)/shard_map/ppermute | solution.py:738
  122.7 2.6 %collective-permute-done.19 = f32[64,64]{1,0:T(8,128)S(1)} collective-permute-done((f32[64,64]{1,0:T(8,128)S(1)}, f32[64,64]{1,0:T(8,128)S(1)}, u32[]{:S(2)}, u32[]{:S(2)}) %collective-permute-start.19) | collective-permute-done | bytes 16416 | tf_op jit(solution)/shard_map/ppermute | solution.py:738
  125.3 6.4 %basis.1 = (f32[16,3456]{1,0:T(8,128)S(1)}, f32[16,3456]{1,0:T(8,128)S(1)}, f32[16,3456]{1,0:T(8,128)S(1)}, f32[16,3456]{1,0:T(8,128)S(1)}) custom-call(f32[64,64]{1,0:T(8,128)S(1)} %add_add_fusion.gram_ref, f32[64,3456]{1,0:T(8,128)S(1)} %get-tuple-element.66.all_ref), custom_call_target="tpu_custom_call" | custom-call | tf_op jit(solution)/shard_map/basis/pallas_call | solution.py:702
  132.0 2.6 %collective-permute-start.22 = (f32[16,3456]{1,0:T(8,128)S(1)}, f32[16,3456]{1,0:T(8,128)S(1)}, u32[]{:S(2)}, u32[]{:S(2)}) collective-permute-start(f32[16,3456]{1,0:T(8,128)S(1)} %get-tuple-element.69), channel_id=1, source_target_pairs={{0,2},{1,3},{2,0},{3,1},{4,6},{5,7},{6,4},{7,5},{8,10},{9,11},{10,... | collective-permute-start | bytes 663560 | tf_op jit(solution)/shard_map/ppermute | solution.py:733
  134.6 1.8 %collective-permute-start.23 = (f32[16,3456]{1,0:T(8,128)S(1)}, f32[16,3456]{1,0:T(8,128)S(1)}, u32[]{:S(2)}, u32[]{:S(2)}) collective-permute-start(f32[16,3456]{1,0:T(8,128)S(1)} %get-tuple-element.70), channel_id=1, source_target_pairs={{0,3},{1,0},{2,1},{3,2},{4,7},{5,4},{6,5},{7,6},{8,11},{9,8},{10,9... | collective-permute-start | bytes 663560 | tf_op jit(solution)/shard_map/ppermute | solution.py:733
  136.4 4.9 %collective-permute-done.21.q1_ref = f32[16,3456]{1,0:T(8,128)S(1)} collective-permute-done((f32[16,3456]{1,0:T(8,128)S(1)}, f32[16,3456]{1,0:T(8,128)S(1)}, u32[]{:S(2)}, u32[]{:S(2)}) %collective-permute-start.21) | collective-permute-done | bytes 221216 | tf_op jit(solution)/shard_map/ppermute | solution.py:733
  (45 shorter events, 20.3 us)
Async XLA Ops:
  2.4 21.5 %collective-permute-start.3 = (f32[72,896]{1,0:T(8,128)}, f32[72,896]{1,0:T(8,128)S(1)}, u32[]{:S(2)}, u32[]{:S(2)}) collective-permute-start(f32[72,896]{1,0:T(8,128)} %get-tuple-element.42.own_ref), channel_id=1, source_target_pairs={{0,124},{4,0},{8,4},{12,8},{16,12},{20,16},{24,20},{28,24},{32,28}... | collective-permute-start | bytes 774152 | tf_op jit(solution)/shard_map/ppermute | solution.py:733
  7.2 16.7 %collective-permute-start.2 = (f32[72,896]{1,0:T(8,128)}, f32[72,896]{1,0:T(8,128)S(1)}, u32[]{:S(2)}, u32[]{:S(2)}) collective-permute-start(f32[72,896]{1,0:T(8,128)} %get-tuple-element.42.own_ref), channel_id=1, source_target_pairs={{0,4},{4,8},{8,12},{12,16},{16,20},{20,24},{24,28},{28,32},{32,36}... | collective-permute-start | bytes 774152 | tf_op jit(solution)/shard_map/ppermute | solution.py:733
  18.7 14.4 %collective-permute-start = (f32[16,768]{1,0:T(8,128)S(1)}, f32[16,768]{1,0:T(8,128)S(1)}, u32[]{:S(2)}, u32[]{:S(2)}) collective-permute-start(f32[16,768]{1,0:T(8,128)S(1)} %get-tuple-element.40), channel_id=1, source_target_pairs={{0,4},{4,8},{8,12},{12,16},{16,20},{20,24},{24,28},{28,32},{32,36}... | collective-permute-start | bytes 147464 | tf_op jit(solution)/shard_map/ppermute | solution.py:733
  18.8 14.3 %collective-permute-start.1 = (f32[16,768]{1,0:T(8,128)S(1)}, f32[16,768]{1,0:T(8,128)S(1)}, u32[]{:S(2)}, u32[]{:S(2)}) collective-permute-start(f32[16,768]{1,0:T(8,128)S(1)} %get-tuple-element.41), channel_id=1, source_target_pairs={{0,124},{4,0},{8,4},{12,8},{16,12},{20,16},{24,20},{28,24},{32,28}... | collective-permute-start | bytes 147464 | tf_op jit(solution)/shard_map/ppermute | solution.py:733
  46.4 6.9 %collective-permute-start.4 = (f32[16,768]{1,0:T(8,128)S(1)}, f32[16,768]{1,0:T(8,128)S(1)}, u32[]{:S(2)}, u32[]{:S(2)}) collective-permute-start(f32[16,768]{1,0:T(8,128)S(1)} %get-tuple-element.56), channel_id=1, source_target_pairs={{0,4},{4,8},{8,12},{12,16},{16,20},{20,24},{24,28},{28,32},{32,36}... | collective-permute-start | bytes 147464 | tf_op jit(solution)/shard_map/ppermute | solution.py:733
  46.5 6.8 %collective-permute-start.5 = (f32[16,768]{1,0:T(8,128)S(1)}, f32[16,768]{1,0:T(8,128)S(1)}, u32[]{:S(2)}, u32[]{:S(2)}) collective-permute-start(f32[16,768]{1,0:T(8,128)S(1)} %get-tuple-element.57), channel_id=1, source_target_pairs={{0,124},{4,0},{8,4},{12,8},{16,12},{20,16},{24,20},{28,24},{32,28}... | collective-permute-start | bytes 147464 | tf_op jit(solution)/shard_map/ppermute | solution.py:733
  66.4 6.9 %collective-permute-start.6 = (f32[16,768]{1,0:T(8,128)S(1)}, f32[16,768]{1,0:T(8,128)S(1)}, u32[]{:S(2)}, u32[]{:S(2)}) collective-permute-start(f32[16,768]{1,0:T(8,128)S(1)} %get-tuple-element.59), channel_id=1, source_target_pairs={{0,4},{4,8},{8,12},{12,16},{16,20},{20,24},{24,28},{28,32},{32,36}... | collective-permute-start | bytes 147464 | tf_op jit(solution)/shard_map/ppermute | solution.py:733
  66.5 6.9 %collective-permute-start.7 = (f32[16,768]{1,0:T(8,128)S(1)}, f32[16,768]{1,0:T(8,128)S(1)}, u32[]{:S(2)}, u32[]{:S(2)}) collective-permute-start(f32[16,768]{1,0:T(8,128)S(1)} %get-tuple-element.60), channel_id=1, source_target_pairs={{0,124},{4,0},{8,4},{12,8},{16,12},{20,16},{24,20},{28,24},{32,28}... | collective-permute-start | bytes 147464 | tf_op jit(solution)/shard_map/ppermute | solution.py:733
  86.8 9.2 %collective-permute-start.8 = (f32[16,3456]{1,0:T(8,128)S(1)}, f32[16,3456]{1,0:T(8,128)S(1)}, u32[]{:S(2)}, u32[]{:S(2)}) collective-permute-start(f32[16,3456]{1,0:T(8,128)S(1)} %get-tuple-element.62), channel_id=1, source_target_pairs={{0,1},{1,2},{2,3},{3,0},{4,5},{5,6},{6,7},{7,4},{8,9},{9,10},{10,1... | collective-permute-start | bytes 663560 | tf_op jit(solution)/shard_map/ppermute | solution.py:733
  88.8 9.9 %collective-permute-start.9 = (f32[16,3456]{1,0:T(8,128)S(1)}, f32[16,3456]{1,0:T(8,128)S(1)}, u32[]{:S(2)}, u32[]{:S(2)}) collective-permute-start(f32[16,3456]{1,0:T(8,128)S(1)} %get-tuple-element.63), channel_id=1, source_target_pairs={{0,2},{1,3},{2,0},{3,1},{4,6},{5,7},{6,4},{7,5},{8,10},{9,11},{10,... | collective-permute-start | bytes 663560 | tf_op jit(solution)/shard_map/ppermute | solution.py:733
  92.4 6.3 %collective-permute-start.10 = (f32[16,3456]{1,0:T(8,128)S(1)}, f32[16,3456]{1,0:T(8,128)S(1)}, u32[]{:S(2)}, u32[]{:S(2)}) collective-permute-start(f32[16,3456]{1,0:T(8,128)S(1)} %get-tuple-element.64), channel_id=1, source_target_pairs={{0,3},{1,0},{2,1},{3,2},{4,7},{5,4},{6,5},{7,6},{8,11},{9,8},{10,9... | collective-permute-start | bytes 663560 | tf_op jit(solution)/shard_map/ppermute | solution.py:733
  99.6 1.3 collective-permute-start.11
  100.9 6.7 %collective-permute-start.14 = (f32[64,64]{1,0:T(8,128)S(1)}, f32[64,64]{1,0:T(8,128)S(1)}, u32[]{:S(2)}, u32[]{:S(2)}) collective-permute-start(f32[64,64]{1,0:T(8,128)S(1)} %add.30), channel_id=1, source_target_pairs={{0,24},{4,28},{8,16},{12,20},{16,8},{20,12},{24,0},{28,4},{32,56},... | collective-permute-start | bytes 49160 | tf_op jit(solution)/shard_map/ppermute | solution.py:738
  105.6 5.4 %collective-permute-start.13 = (f32[64,64]{1,0:T(8,128)S(1)}, f32[64,64]{1,0:T(8,128)S(1)}, u32[]{:S(2)}, u32[]{:S(2)}) collective-permute-start(f32[64,64]{1,0:T(8,128)S(1)} %add.30), channel_id=1, source_target_pairs={{0,16},{4,20},{8,24},{12,28},{16,0},{20,4},{24,8},{28,12},{32,48},... | collective-permute-start | bytes 49160 | tf_op jit(solution)/shard_map/ppermute | solution.py:738
  105.6 5.4 %collective-permute-start.12 = (f32[64,64]{1,0:T(8,128)S(1)}, f32[64,64]{1,0:T(8,128)S(1)}, u32[]{:S(2)}, u32[]{:S(2)}) collective-permute-start(f32[64,64]{1,0:T(8,128)S(1)} %add.30), channel_id=1, source_target_pairs={{0,8},{4,12},{8,0},{12,4},{16,24},{20,28},{24,16},{28,20},{32,40},... | collective-permute-start | bytes 49160 | tf_op jit(solution)/shard_map/ppermute | solution.py:738
  111.0 5.2 %collective-permute-start.17 = (f32[64,64]{1,0:T(8,128)S(1)}, f32[64,64]{1,0:T(8,128)S(1)}, u32[]{:S(2)}, u32[]{:S(2)}) collective-permute-start(f32[64,64]{1,0:T(8,128)S(1)} %add_add_fusion.2), channel_id=1, source_target_pairs={{0,96},{4,100},{8,104},{12,108},{16,112},{20,116},{24,120},{28,124... | collective-permute-start | bytes 49160 | tf_op jit(solution)/shard_map/ppermute | solution.py:738
  111.5 5.4 %collective-permute-start.16 = (f32[64,64]{1,0:T(8,128)S(1)}, f32[64,64]{1,0:T(8,128)S(1)}, u32[]{:S(2)}, u32[]{:S(2)}) collective-permute-start(f32[64,64]{1,0:T(8,128)S(1)} %add_add_fusion.2), channel_id=1, source_target_pairs={{0,64},{4,68},{8,72},{12,76},{16,80},{20,84},{24,88},{28,92},{32,9... | collective-permute-start | bytes 49160 | tf_op jit(solution)/shard_map/ppermute | solution.py:738
  113.1 4.4 %collective-permute-start.15 = (f32[64,64]{1,0:T(8,128)S(1)}, f32[64,64]{1,0:T(8,128)S(1)}, u32[]{:S(2)}, u32[]{:S(2)}) collective-permute-start(f32[64,64]{1,0:T(8,128)S(1)} %add_add_fusion.2), channel_id=1, source_target_pairs={{0,32},{4,36},{8,40},{12,44},{16,48},{20,52},{24,56},{28,60},{32,0... | collective-permute-start | bytes 49160 | tf_op jit(solution)/shard_map/ppermute | solution.py:738
  117.5 5.2 %collective-permute-start.20 = (f32[64,64]{1,0:T(8,128)S(1)}, f32[64,64]{1,0:T(8,128)S(1)}, u32[]{:S(2)}, u32[]{:S(2)}) collective-permute-start(f32[64,64]{1,0:T(8,128)S(1)} %add_add_fusion.1), channel_id=1, source_target_pairs={{0,3},{1,2},{2,1},{3,0},{4,7},{5,6},{6,5},{7,4},{8,11},{9,10},{10,... | collective-permute-start | bytes 49160 | tf_op jit(solution)/shard_map/ppermute | solution.py:738
  119.9 5.4 %collective-permute-start.19 = (f32[64,64]{1,0:T(8,128)S(1)}, f32[64,64]{1,0:T(8,128)S(1)}, u32[]{:S(2)}, u32[]{:S(2)}) collective-permute-start(f32[64,64]{1,0:T(8,128)S(1)} %add_add_fusion.1), channel_id=1, source_target_pairs={{0,2},{1,3},{2,0},{3,1},{4,6},{5,7},{6,4},{7,5},{8,10},{9,11},{10,... | collective-permute-start | bytes 49160 | tf_op jit(solution)/shard_map/ppermute | solution.py:738
  121.1 4.2 %collective-permute-start.18 = (f32[64,64]{1,0:T(8,128)S(1)}, f32[64,64]{1,0:T(8,128)S(1)}, u32[]{:S(2)}, u32[]{:S(2)}) collective-permute-start(f32[64,64]{1,0:T(8,128)S(1)} %add_add_fusion.1), channel_id=1, source_target_pairs={{0,1},{1,0},{2,3},{3,2},{4,5},{5,4},{6,7},{7,6},{8,9},{9,8},{10,11... | collective-permute-start | bytes 49160 | tf_op jit(solution)/shard_map/ppermute | solution.py:738
  131.7 9.6 %collective-permute-start.21 = (f32[16,3456]{1,0:T(8,128)S(1)}, f32[16,3456]{1,0:T(8,128)S(1)}, u32[]{:S(2)}, u32[]{:S(2)}) collective-permute-start(f32[16,3456]{1,0:T(8,128)S(1)} %get-tuple-element.68), channel_id=1, source_target_pairs={{0,1},{1,2},{2,3},{3,0},{4,5},{5,6},{6,7},{7,4},{8,9},{9,10},{10,1... | collective-permute-start | bytes 663560 | tf_op jit(solution)/shard_map/ppermute | solution.py:733
  132.0 9.3 %collective-permute-start.22 = (f32[16,3456]{1,0:T(8,128)S(1)}, f32[16,3456]{1,0:T(8,128)S(1)}, u32[]{:S(2)}, u32[]{:S(2)}) collective-permute-start(f32[16,3456]{1,0:T(8,128)S(1)} %get-tuple-element.69), channel_id=1, source_target_pairs={{0,2},{1,3},{2,0},{3,1},{4,6},{5,7},{6,4},{7,5},{8,10},{9,11},{10,... | collective-permute-start | bytes 663560 | tf_op jit(solution)/shard_map/ppermute | solution.py:733
  134.6 7.5 %collective-permute-start.23 = (f32[16,3456]{1,0:T(8,128)S(1)}, f32[16,3456]{1,0:T(8,128)S(1)}, u32[]{:S(2)}, u32[]{:S(2)}) collective-permute-start(f32[16,3456]{1,0:T(8,128)S(1)} %get-tuple-element.70), channel_id=1, source_target_pairs={{0,3},{1,0},{2,1},{3,2},{4,7},{5,4},{6,5},{7,6},{8,11},{9,8},{10,9... | collective-permute-start | bytes 663560 | tf_op jit(solution)/shard_map/ppermute | solution.py:733
  (4 other events, 4.0 us)

commit v3 on v2

--- a/solution.py
+++ b/solution.py
@@ -136,7 +136,7 @@
     return pl.ds(pl.multiple_of((c // QB) * S, S), S), pl.ds(pl.multiple_of((c % QB) * L, L), L)
 
 
-UNROLL = 12
+UNROLL = 18
 
 
 def compress(read, z_ref, src_ref, start_ref):

time: 143 us -> 143 us (level); the launches traced: 143 us -> 142 us
  Pallas kernels: 66.5 us -> 60.4 us
  starting transfers between devices: 45.8 us -> 50.4 us
    pallas_call x3, Pallas kernels: 39.9 us -> 35 us  [apply_step(): pl.pallas_call(functools.partial(step_kernel, number), out_shape=shapes,...]
    ppermute x10, starting transfers between devices: 14.1 us -> 17.4 us  [swap(): return lax.ppermute(x, axis, [(i, i ^ bits) for i in range(size)])]
  transfers between devices with their start and end apart: 24 -> 24, of which waited for: 15 -> 15; matrix products, arithmetic and copies ran while one was open for 0% -> 0% of each run, Pallas kernels for 12% -> 11%
where the time goes in v3:
time: 143 us; the launch traced here: 142 us
  Pallas kernels  60.4 us (42%)
  starting transfers between devices  50.4 us (35%)
  waiting for transfers between devices  26 us (18%)
  local copies, waits for them, and re-layouts  3.98 us (3%)
    pallas_call x3, Pallas kernels, apply_step(): pl.pallas_call(functools.partial(step_kernel, number), out_shape=shapes,...  35 us
    ppermute x14, starting transfers between devices, shift(): return lax.ppermute(x, axis, [(i, (i + by) % size) for i in range(size)])  33 us
    ppermute x10, starting transfers between devices, swap(): return lax.ppermute(x, axis, [(i, i ^ bits) for i in range(size)])  17.4 us
    ppermute x14, waiting for transfers between devices, shift(): return lax.ppermute(x, axis, [(i, (i + by) % size) for i in range(size)])  14.5 us
    ppermute x10, waiting for transfers between devices, swap(): return lax.ppermute(x, axis, [(i, i ^ bits) for i in range(size)])  11.5 us
    pallas_call x1, Pallas kernels, prepare(): pl.pallas_call(prepare_kernel, out_shape=(sds((1, E), I32), sds((1, ME)),...  9.13 us
    pallas_call x1, Pallas kernels, basis_of(): pl.pallas_call(functools.partial(basis_kernel, total), out_shape=(sds((S,...  6.38 us
    pallas_call x1, Pallas kernels, cell_tables(): pl.pallas_call(cells_kernel, out_shape=(sds((SLOTS, 16, L), I32), sds((SL...  6.29 us
  transfers between devices with their start and end apart: 24, of which 15 were waited for; matrix products, arithmetic and copies ran while one was open for 0% of the time, Pallas kernels for 11%

profile of v3, /device:TPU:0, one launch (start us, length us, event | category | flops | bytes accessed | tf_op | source)
XLA Modules:
  0.0 141.6 jit_solution(1723080588438402561)
XLA Ops:
  0.7 1.7 %pack.1 = (f32[72,896]{1,0:T(8,128)}, f32[9,896]{1,0:T(8,128)}) custom-call(s32[64,343]{1,0:T(8,128)} %bitcast.2, f32[64,343]{1,0:T(8,128)} %bitcast.3, f32[64]{0:T(128)} %scale_hbm.1, s32[864]{0:T(1024)} %rows_hbm.1, s32[4,864]{1,0:T(4,128)} %masters_hbm.1, f32[4,864]{1,0:T(4,128)} %weights_hbm.1, s32[1]{0:T(128)S(6)} %copy.10.count_ref), custom_call_target="tpu_custom_call" | custom-call | tf_op jit(solution)/shard_map/pack/pallas_call | solution.py:337
  2.4 4.8 %collective-permute-start.3 = (f32[72,896]{1,0:T(8,128)}, f32[72,896]{1,0:T(8,128)S(1)}, u32[]{:S(2)}, u32[]{:S(2)}) collective-permute-start(f32[72,896]{1,0:T(8,128)} %get-tuple-element.42.own_ref), channel_id=1, source_target_pairs={{0,124},{4,0},{8,4},{12,8},{16,12},{20,16},{24,20},{28,24},{32,28}... | collective-permute-start | bytes 774152 | tf_op jit(solution)/shard_map/ppermute | solution.py:733
  9.2 9.1 %prepare.1 = (s32[1,4608]{1,0:T(1,128)S(1)}, f32[1,3584]{1,0:T(1,128)S(1)}, s32[40,128]{1,0:T(8,128)S(1)}, s32[128,128]{1,0:T(8,128)S(1)}, f32[16,512]{1,0:T(8,1...) custom-call(f32[9,896]{1,0:T(8,128)S(1)} %copy-done.3, ...), custom_call_target="tpu_custom_call" | custom-call | tf_op jit(solution)/shard_map/prepare/pallas_call | solution.py:277
  18.4 5.1 %collective-permute-start.1 = (f32[16,768]{1,0:T(8,128)S(1)}, f32[16,768]{1,0:T(8,128)S(1)}, u32[]{:S(2)}, u32[]{:S(2)}) collective-permute-start(f32[16,768]{1,0:T(8,128)S(1)} %get-tuple-element.41), channel_id=1, source_target_pairs={{0,124},{4,0},{8,4},{12,8},{16,12},{20,16},{24,20},{28,24},{32,28}... | collective-permute-start | bytes 147464 | tf_op jit(solution)/shard_map/ppermute | solution.py:733
  25.5 6.3 %cell_tables.1 = (s32[224,16,128]{2,1,0:T(8,128)S(1)}, f32[224,8,128]{2,1,0:T(8,128)S(1)}, bf16[384,384]{1,0:T(8,128)(2,1)S(1)}, bf16[384,384]{1,0:T(8,128)(2,1)...) custom-call(f32[72,896]{1,0:T(8,128)S(1)} %copy-done.2, f32[72,896]{1,0:T(8,128)S(1)} %collective-permute-done.2.left_ref, ...), custom_call_target="tpu_custom_call" | custom-call | tf_op jit(solution)/shard_map/cell_tables/pallas_call | solution.py:474
  31.8 11.7 %step1.1 = (f32[16,13824]{1,0:T(8,128)S(1)}, f32[16,768]{1,0:T(8,128)S(1)}, f32[16,768]{1,0:T(8,128)S(1)}) custom-call(f32[16,13824]{1,0:T(8,128)S(1)} %get-tuple-element.39.refs_0_.refs_3_, f32[16,768]{1,0:T(8,128)S(1)} %collective-permute-done.refs_1_, f32[16,768]{1,0:T(8,128)S(1)} %collective-permute-done.1.refs_2_, ...), custom_call_target="tpu_custom_call" | custom-call | tf_op jit(solution)/shard_map/step1/pallas_call | solution.py:644
  43.6 5.1 %collective-permute-start.5 = (f32[16,768]{1,0:T(8,128)S(1)}, f32[16,768]{1,0:T(8,128)S(1)}, u32[]{:S(2)}, u32[]{:S(2)}) collective-permute-start(f32[16,768]{1,0:T(8,128)S(1)} %get-tuple-element.57), channel_id=1, source_target_pairs={{0,124},{4,0},{8,4},{12,8},{16,12},{20,16},{24,20},{28,24},{32,28}... | collective-permute-start | bytes 147464 | tf_op jit(solution)/shard_map/ppermute | solution.py:733
  48.7 1.8 %collective-permute-done.4.refs_1_ = f32[16,768]{1,0:T(8,128)S(1)} collective-permute-done((f32[16,768]{1,0:T(8,128)S(1)}, f32[16,768]{1,0:T(8,128)S(1)}, u32[]{:S(2)}, u32[]{:S(2)}) %collective-permute-start.4) | collective-permute-done | bytes 49184 | tf_op jit(solution)/shard_map/ppermute | solution.py:733
  50.4 11.5 %step2.1 = (f32[16,13824]{1,0:T(8,128)S(1)}, f32[16,768]{1,0:T(8,128)S(1)}, f32[16,768]{1,0:T(8,128)S(1)}) custom-call(f32[16,13824]{1,0:T(8,128)S(1)} %get-tuple-element.55.refs_0_.refs_3_, f32[16,768]{1,0:T(8,128)S(1)} %collective-permute-done.4.refs_1_, f32[16,768]{1,0:T(8,128)S(1)} %collective-permute-done.5.refs_2_, ...), custom_call_target="tpu_custom_call" | custom-call | tf_op jit(solution)/shard_map/step2/pallas_call | solution.py:644
  62.1 6.5 %collective-permute-start.7 = (f32[16,768]{1,0:T(8,128)S(1)}, f32[16,768]{1,0:T(8,128)S(1)}, u32[]{:S(2)}, u32[]{:S(2)}) collective-permute-start(f32[16,768]{1,0:T(8,128)S(1)} %get-tuple-element.60), channel_id=1, source_target_pairs={{0,124},{4,0},{8,4},{12,8},{16,12},{20,16},{24,20},{28,24},{32,28}... | collective-permute-start | bytes 147464 | tf_op jit(solution)/shard_map/ppermute | solution.py:733
  68.6 1.7 %collective-permute-done.6.refs_1_ = f32[16,768]{1,0:T(8,128)S(1)} collective-permute-done((f32[16,768]{1,0:T(8,128)S(1)}, f32[16,768]{1,0:T(8,128)S(1)}, u32[]{:S(2)}, u32[]{:S(2)}) %collective-permute-start.6) | collective-permute-done | bytes 49184 | tf_op jit(solution)/shard_map/ppermute | solution.py:733
  70.3 11.8 %step3.1 = (f32[16,3456]{1,0:T(8,128)S(1)}, f32[16,3456]{1,0:T(8,128)S(1)}, f32[16,3456]{1,0:T(8,128)S(1)}, f32[16,3456]{1,0:T(8,128)S(1)}) custom-call(f32[16,13824]{1,0:T(8,128)S(1)} %get-tuple-element.58.refs_0_, f32[16,768]{1,0:T(8,128)S(1)} %collective-permute-done.6.refs_1_, f32[16,768]{1,0:T(8,128)S(1)} %collective-permute-done.7.refs_2_, ...), custom_call_target="tpu_custom_call" | custom-call | tf_op jit(solution)/shard_map/step3/pallas_call | solution.py:644
  82.1 2.0 %collective-permute-start.8 = (f32[16,3456]{1,0:T(8,128)S(1)}, f32[16,3456]{1,0:T(8,128)S(1)}, u32[]{:S(2)}, u32[]{:S(2)}) collective-permute-start(f32[16,3456]{1,0:T(8,128)S(1)} %get-tuple-element.62), channel_id=1, source_target_pairs={{0,1},{1,2},{2,3},{3,0},{4,5},{5,6},{6,7},{7,4},{8,9},{9,10},{10,1... | collective-permute-start | bytes 663560 | tf_op jit(solution)/shard_map/ppermute | solution.py:733
  84.1 3.6 %collective-permute-start.9 = (f32[16,3456]{1,0:T(8,128)S(1)}, f32[16,3456]{1,0:T(8,128)S(1)}, u32[]{:S(2)}, u32[]{:S(2)}) collective-permute-start(f32[16,3456]{1,0:T(8,128)S(1)} %get-tuple-element.63), channel_id=1, source_target_pairs={{0,2},{1,3},{2,0},{3,1},{4,6},{5,7},{6,4},{7,5},{8,10},{9,11},{10,... | collective-permute-start | bytes 663560 | tf_op jit(solution)/shard_map/ppermute | solution.py:733
  90.1 3.8 %collective-permute-done.9.q2_ref = f32[16,3456]{1,0:T(8,128)S(1)} collective-permute-done((f32[16,3456]{1,0:T(8,128)S(1)}, f32[16,3456]{1,0:T(8,128)S(1)}, u32[]{:S(2)}, u32[]{:S(2)}) %collective-permute-start.9) | collective-permute-done | bytes 221216 | tf_op jit(solution)/shard_map/ppermute | solution.py:733
  96.1 8.1 %collective-permute-start.14 = (f32[64,64]{1,0:T(8,128)S(1)}, f32[64,64]{1,0:T(8,128)S(1)}, u32[]{:S(2)}, u32[]{:S(2)}) collective-permute-start(f32[64,64]{1,0:T(8,128)S(1)} %add.30), channel_id=1, source_target_pairs={{0,24},{4,28},{8,16},{12,20},{16,8},{20,12},{24,0},{28,4},{32,56},... | collective-permute-start | bytes 49160 | tf_op jit(solution)/shard_map/ppermute | solution.py:738
  106.1 3.5 %collective-permute-done.13 = f32[64,64]{1,0:T(8,128)S(1)} collective-permute-done((f32[64,64]{1,0:T(8,128)S(1)}, f32[64,64]{1,0:T(8,128)S(1)}, u32[]{:S(2)}, u32[]{:S(2)}) %collective-permute-start.13) | collective-permute-done | bytes 16416 | tf_op jit(solution)/shard_map/ppermute | solution.py:738
  109.7 2.5 %collective-permute-start.16 = (f32[64,64]{1,0:T(8,128)S(1)}, f32[64,64]{1,0:T(8,128)S(1)}, u32[]{:S(2)}, u32[]{:S(2)}) collective-permute-start(f32[64,64]{1,0:T(8,128)S(1)} %add_add_fusion.2), channel_id=1, source_target_pairs={{0,64},{4,68},{8,72},{12,76},{16,80},{20,84},{24,88},{28,92},{32,9... | collective-permute-start | bytes 49160 | tf_op jit(solution)/shard_map/ppermute | solution.py:738
  116.2 2.2 %collective-permute-start.20 = (f32[64,64]{1,0:T(8,128)S(1)}, f32[64,64]{1,0:T(8,128)S(1)}, u32[]{:S(2)}, u32[]{:S(2)}) collective-permute-start(f32[64,64]{1,0:T(8,128)S(1)} %add_add_fusion.1), channel_id=1, source_target_pairs={{0,3},{1,2},{2,1},{3,0},{4,7},{5,6},{6,5},{7,4},{8,11},{9,10},{10,... | collective-permute-start | bytes 49160 | tf_op jit(solution)/shard_map/ppermute | solution.py:738
  121.4 2.5 %collective-permute-done.19 = f32[64,64]{1,0:T(8,128)S(1)} collective-permute-done((f32[64,64]{1,0:T(8,128)S(1)}, f32[64,64]{1,0:T(8,128)S(1)}, u32[]{:S(2)}, u32[]{:S(2)}) %collective-permute-start.19) | collective-permute-done | bytes 16416 | tf_op jit(solution)/shard_map/ppermute | solution.py:738
  123.8 6.4 %basis.1 = (f32[16,3456]{1,0:T(8,128)S(1)}, f32[16,3456]{1,0:T(8,128)S(1)}, f32[16,3456]{1,0:T(8,128)S(1)}, f32[16,3456]{1,0:T(8,128)S(1)}) custom-call(f32[64,64]{1,0:T(8,128)S(1)} %add_add_fusion.gram_ref, f32[64,3456]{1,0:T(8,128)S(1)} %get-tuple-element.66.all_ref), custom_call_target="tpu_custom_call" | custom-call | tf_op jit(solution)/shard_map/basis/pallas_call | solution.py:702
  130.7 2.5 %collective-permute-start.22 = (f32[16,3456]{1,0:T(8,128)S(1)}, f32[16,3456]{1,0:T(8,128)S(1)}, u32[]{:S(2)}, u32[]{:S(2)}) collective-permute-start(f32[16,3456]{1,0:T(8,128)S(1)} %get-tuple-element.69), channel_id=1, source_target_pairs={{0,2},{1,3},{2,0},{3,1},{4,6},{5,7},{6,4},{7,5},{8,10},{9,11},{10,... | collective-permute-start | bytes 663560 | tf_op jit(solution)/shard_map/ppermute | solution.py:733
  133.2 1.7 %collective-permute-start.23 = (f32[16,3456]{1,0:T(8,128)S(1)}, f32[16,3456]{1,0:T(8,128)S(1)}, u32[]{:S(2)}, u32[]{:S(2)}) collective-permute-start(f32[16,3456]{1,0:T(8,128)S(1)} %get-tuple-element.70), channel_id=1, source_target_pairs={{0,3},{1,0},{2,1},{3,2},{4,7},{5,4},{6,5},{7,6},{8,11},{9,8},{10,9... | collective-permute-start | bytes 663560 | tf_op jit(solution)/shard_map/ppermute | solution.py:733
  134.9 4.9 %collective-permute-done.21.q1_ref = f32[16,3456]{1,0:T(8,128)S(1)} collective-permute-done((f32[16,3456]{1,0:T(8,128)S(1)}, f32[16,3456]{1,0:T(8,128)S(1)}, u32[]{:S(2)}, u32[]{:S(2)}) %collective-permute-start.21) | collective-permute-done | bytes 221216 | tf_op jit(solution)/shard_map/ppermute | solution.py:733
  (45 shorter events, 20.1 us)
Async XLA Ops:
  2.4 21.1 %collective-permute-start.3 = (f32[72,896]{1,0:T(8,128)}, f32[72,896]{1,0:T(8,128)S(1)}, u32[]{:S(2)}, u32[]{:S(2)}) collective-permute-start(f32[72,896]{1,0:T(8,128)} %get-tuple-element.42.own_ref), channel_id=1, source_target_pairs={{0,124},{4,0},{8,4},{12,8},{16,12},{20,16},{24,20},{28,24},{32,28}... | collective-permute-start | bytes 774152 | tf_op jit(solution)/shard_map/ppermute | solution.py:733
  7.2 16.3 %collective-permute-start.2 = (f32[72,896]{1,0:T(8,128)}, f32[72,896]{1,0:T(8,128)S(1)}, u32[]{:S(2)}, u32[]{:S(2)}) collective-permute-start(f32[72,896]{1,0:T(8,128)} %get-tuple-element.42.own_ref), channel_id=1, source_target_pairs={{0,4},{4,8},{8,12},{12,16},{16,20},{20,24},{24,28},{28,32},{32,36}... | collective-permute-start | bytes 774152 | tf_op jit(solution)/shard_map/ppermute | solution.py:733
  18.3 13.5 %collective-permute-start = (f32[16,768]{1,0:T(8,128)S(1)}, f32[16,768]{1,0:T(8,128)S(1)}, u32[]{:S(2)}, u32[]{:S(2)}) collective-permute-start(f32[16,768]{1,0:T(8,128)S(1)} %get-tuple-element.40), channel_id=1, source_target_pairs={{0,4},{4,8},{8,12},{12,16},{16,20},{20,24},{24,28},{28,32},{32,36}... | collective-permute-start | bytes 147464 | tf_op jit(solution)/shard_map/ppermute | solution.py:733
  18.4 13.4 %collective-permute-start.1 = (f32[16,768]{1,0:T(8,128)S(1)}, f32[16,768]{1,0:T(8,128)S(1)}, u32[]{:S(2)}, u32[]{:S(2)}) collective-permute-start(f32[16,768]{1,0:T(8,128)S(1)} %get-tuple-element.41), channel_id=1, source_target_pairs={{0,124},{4,0},{8,4},{12,8},{16,12},{20,16},{24,20},{28,24},{32,28}... | collective-permute-start | bytes 147464 | tf_op jit(solution)/shard_map/ppermute | solution.py:733
  43.5 6.9 %collective-permute-start.4 = (f32[16,768]{1,0:T(8,128)S(1)}, f32[16,768]{1,0:T(8,128)S(1)}, u32[]{:S(2)}, u32[]{:S(2)}) collective-permute-start(f32[16,768]{1,0:T(8,128)S(1)} %get-tuple-element.56), channel_id=1, source_target_pairs={{0,4},{4,8},{8,12},{12,16},{16,20},{20,24},{24,28},{28,32},{32,36}... | collective-permute-start | bytes 147464 | tf_op jit(solution)/shard_map/ppermute | solution.py:733
  43.6 6.8 %collective-permute-start.5 = (f32[16,768]{1,0:T(8,128)S(1)}, f32[16,768]{1,0:T(8,128)S(1)}, u32[]{:S(2)}, u32[]{:S(2)}) collective-permute-start(f32[16,768]{1,0:T(8,128)S(1)} %get-tuple-element.57), channel_id=1, source_target_pairs={{0,124},{4,0},{8,4},{12,8},{16,12},{20,16},{24,20},{28,24},{32,28}... | collective-permute-start | bytes 147464 | tf_op jit(solution)/shard_map/ppermute | solution.py:733
  62.0 8.3 %collective-permute-start.6 = (f32[16,768]{1,0:T(8,128)S(1)}, f32[16,768]{1,0:T(8,128)S(1)}, u32[]{:S(2)}, u32[]{:S(2)}) collective-permute-start(f32[16,768]{1,0:T(8,128)S(1)} %get-tuple-element.59), channel_id=1, source_target_pairs={{0,4},{4,8},{8,12},{12,16},{16,20},{20,24},{24,28},{28,32},{32,36}... | collective-permute-start | bytes 147464 | tf_op jit(solution)/shard_map/ppermute | solution.py:733
  62.1 8.2 %collective-permute-start.7 = (f32[16,768]{1,0:T(8,128)S(1)}, f32[16,768]{1,0:T(8,128)S(1)}, u32[]{:S(2)}, u32[]{:S(2)}) collective-permute-start(f32[16,768]{1,0:T(8,128)S(1)} %get-tuple-element.60), channel_id=1, source_target_pairs={{0,124},{4,0},{8,4},{12,8},{16,12},{20,16},{24,20},{28,24},{32,28}... | collective-permute-start | bytes 147464 | tf_op jit(solution)/shard_map/ppermute | solution.py:733
  82.1 8.0 %collective-permute-start.8 = (f32[16,3456]{1,0:T(8,128)S(1)}, f32[16,3456]{1,0:T(8,128)S(1)}, u32[]{:S(2)}, u32[]{:S(2)}) collective-permute-start(f32[16,3456]{1,0:T(8,128)S(1)} %get-tuple-element.62), channel_id=1, source_target_pairs={{0,1},{1,2},{2,3},{3,0},{4,5},{5,6},{6,7},{7,4},{8,9},{9,10},{10,1... | collective-permute-start | bytes 663560 | tf_op jit(solution)/shard_map/ppermute | solution.py:733
  84.1 9.9 %collective-permute-start.9 = (f32[16,3456]{1,0:T(8,128)S(1)}, f32[16,3456]{1,0:T(8,128)S(1)}, u32[]{:S(2)}, u32[]{:S(2)}) collective-permute-start(f32[16,3456]{1,0:T(8,128)S(1)} %get-tuple-element.63), channel_id=1, source_target_pairs={{0,2},{1,3},{2,0},{3,1},{4,6},{5,7},{6,4},{7,5},{8,10},{9,11},{10,... | collective-permute-start | bytes 663560 | tf_op jit(solution)/shard_map/ppermute | solution.py:733
  87.7 6.3 %collective-permute-start.10 = (f32[16,3456]{1,0:T(8,128)S(1)}, f32[16,3456]{1,0:T(8,128)S(1)}, u32[]{:S(2)}, u32[]{:S(2)}) collective-permute-start(f32[16,3456]{1,0:T(8,128)S(1)} %get-tuple-element.64), channel_id=1, source_target_pairs={{0,3},{1,0},{2,1},{3,2},{4,7},{5,4},{6,5},{7,6},{8,11},{9,8},{10,9... | collective-permute-start | bytes 663560 | tf_op jit(solution)/shard_map/ppermute | solution.py:733
  94.8 1.3 collective-permute-start.11
  96.1 10.0 %collective-permute-start.14 = (f32[64,64]{1,0:T(8,128)S(1)}, f32[64,64]{1,0:T(8,128)S(1)}, u32[]{:S(2)}, u32[]{:S(2)}) collective-permute-start(f32[64,64]{1,0:T(8,128)S(1)} %add.30), channel_id=1, source_target_pairs={{0,24},{4,28},{8,16},{12,20},{16,8},{20,12},{24,0},{28,4},{32,56},... | collective-permute-start | bytes 49160 | tf_op jit(solution)/shard_map/ppermute | solution.py:738
  104.2 5.4 %collective-permute-start.13 = (f32[64,64]{1,0:T(8,128)S(1)}, f32[64,64]{1,0:T(8,128)S(1)}, u32[]{:S(2)}, u32[]{:S(2)}) collective-permute-start(f32[64,64]{1,0:T(8,128)S(1)} %add.30), channel_id=1, source_target_pairs={{0,16},{4,20},{8,24},{12,28},{16,0},{20,4},{24,8},{28,12},{32,48},... | collective-permute-start | bytes 49160 | tf_op jit(solution)/shard_map/ppermute | solution.py:738
  104.2 5.4 %collective-permute-start.12 = (f32[64,64]{1,0:T(8,128)S(1)}, f32[64,64]{1,0:T(8,128)S(1)}, u32[]{:S(2)}, u32[]{:S(2)}) collective-permute-start(f32[64,64]{1,0:T(8,128)S(1)} %add.30), channel_id=1, source_target_pairs={{0,8},{4,12},{8,0},{12,4},{16,24},{20,28},{24,16},{28,20},{32,40},... | collective-permute-start | bytes 49160 | tf_op jit(solution)/shard_map/ppermute | solution.py:738
  109.6 5.2 %collective-permute-start.17 = (f32[64,64]{1,0:T(8,128)S(1)}, f32[64,64]{1,0:T(8,128)S(1)}, u32[]{:S(2)}, u32[]{:S(2)}) collective-permute-start(f32[64,64]{1,0:T(8,128)S(1)} %add_add_fusion.2), channel_id=1, source_target_pairs={{0,96},{4,100},{8,104},{12,108},{16,112},{20,116},{24,120},{28,124... | collective-permute-start | bytes 49160 | tf_op jit(solution)/shard_map/ppermute | solution.py:738
  109.7 5.5 %collective-permute-start.16 = (f32[64,64]{1,0:T(8,128)S(1)}, f32[64,64]{1,0:T(8,128)S(1)}, u32[]{:S(2)}, u32[]{:S(2)}) collective-permute-start(f32[64,64]{1,0:T(8,128)S(1)} %add_add_fusion.2), channel_id=1, source_target_pairs={{0,64},{4,68},{8,72},{12,76},{16,80},{20,84},{24,88},{28,92},{32,9... | collective-permute-start | bytes 49160 | tf_op jit(solution)/shard_map/ppermute | solution.py:738
  112.2 3.9 %collective-permute-start.15 = (f32[64,64]{1,0:T(8,128)S(1)}, f32[64,64]{1,0:T(8,128)S(1)}, u32[]{:S(2)}, u32[]{:S(2)}) collective-permute-start(f32[64,64]{1,0:T(8,128)S(1)} %add_add_fusion.2), channel_id=1, source_target_pairs={{0,32},{4,36},{8,40},{12,44},{16,48},{20,52},{24,56},{28,60},{32,0... | collective-permute-start | bytes 49160 | tf_op jit(solution)/shard_map/ppermute | solution.py:738
  116.2 5.2 %collective-permute-start.20 = (f32[64,64]{1,0:T(8,128)S(1)}, f32[64,64]{1,0:T(8,128)S(1)}, u32[]{:S(2)}, u32[]{:S(2)}) collective-permute-start(f32[64,64]{1,0:T(8,128)S(1)} %add_add_fusion.1), channel_id=1, source_target_pairs={{0,3},{1,2},{2,1},{3,0},{4,7},{5,6},{6,5},{7,4},{8,11},{9,10},{10,... | collective-permute-start | bytes 49160 | tf_op jit(solution)/shard_map/ppermute | solution.py:738
  118.4 5.4 %collective-permute-start.19 = (f32[64,64]{1,0:T(8,128)S(1)}, f32[64,64]{1,0:T(8,128)S(1)}, u32[]{:S(2)}, u32[]{:S(2)}) collective-permute-start(f32[64,64]{1,0:T(8,128)S(1)} %add_add_fusion.1), channel_id=1, source_target_pairs={{0,2},{1,3},{2,0},{3,1},{4,6},{5,7},{6,4},{7,5},{8,10},{9,11},{10,... | collective-permute-start | bytes 49160 | tf_op jit(solution)/shard_map/ppermute | solution.py:738
  119.8 4.0 %collective-permute-start.18 = (f32[64,64]{1,0:T(8,128)S(1)}, f32[64,64]{1,0:T(8,128)S(1)}, u32[]{:S(2)}, u32[]{:S(2)}) collective-permute-start(f32[64,64]{1,0:T(8,128)S(1)} %add_add_fusion.1), channel_id=1, source_target_pairs={{0,1},{1,0},{2,3},{3,2},{4,5},{5,4},{6,7},{7,6},{8,9},{9,8},{10,11... | collective-permute-start | bytes 49160 | tf_op jit(solution)/shard_map/ppermute | solution.py:738
  130.2 9.6 %collective-permute-start.21 = (f32[16,3456]{1,0:T(8,128)S(1)}, f32[16,3456]{1,0:T(8,128)S(1)}, u32[]{:S(2)}, u32[]{:S(2)}) collective-permute-start(f32[16,3456]{1,0:T(8,128)S(1)} %get-tuple-element.68), channel_id=1, source_target_pairs={{0,1},{1,2},{2,3},{3,0},{4,5},{5,6},{6,7},{7,4},{8,9},{9,10},{10,1... | collective-permute-start | bytes 663560 | tf_op jit(solution)/shard_map/ppermute | solution.py:733
  130.7 9.1 %collective-permute-start.22 = (f32[16,3456]{1,0:T(8,128)S(1)}, f32[16,3456]{1,0:T(8,128)S(1)}, u32[]{:S(2)}, u32[]{:S(2)}) collective-permute-start(f32[16,3456]{1,0:T(8,128)S(1)} %get-tuple-element.69), channel_id=1, source_target_pairs={{0,2},{1,3},{2,0},{3,1},{4,6},{5,7},{6,4},{7,5},{8,10},{9,11},{10,... | collective-permute-start | bytes 663560 | tf_op jit(solution)/shard_map/ppermute | solution.py:733
  133.2 7.4 %collective-permute-start.23 = (f32[16,3456]{1,0:T(8,128)S(1)}, f32[16,3456]{1,0:T(8,128)S(1)}, u32[]{:S(2)}, u32[]{:S(2)}) collective-permute-start(f32[16,3456]{1,0:T(8,128)S(1)} %get-tuple-element.70), channel_id=1, source_target_pairs={{0,3},{1,0},{2,1},{3,2},{4,7},{5,4},{6,5},{7,6},{8,11},{9,8},{10,9... | collective-permute-start | bytes 663560 | tf_op jit(solution)/shard_map/ppermute | solution.py:733
  (4 other events, 4.0 us)
